TPU v7x, 128 devices: a whole 4x4x4 slice. The times are simulated.
128 devices in a mesh: rx: 32 (over y, z, core), ry: 4 (over x).
Axes of the slice: x: 4, y: 4, z: 4, core: 2. Of those that a mesh axis runs over, the one named last changes fastest.
Arguments:
- matrix: float32 [524288, 256], P(('rx', 'ry')), may hold values from -6 to 6
- signs: int32 [524288], P(('rx', 'ry')), may hold values from -1 to 1, as said below
- indices: int32 [32768], P(('rx', 'ry')), may hold values from 0 to 4095, as said below
- counts: int32 [128], P(('rx', 'ry')), may hold values from 64 to 256, as said below
Outputs:
- sketch: float32 [32768, 256], P(('rx', 'ry'))
- gram_blocks: float32 [4, 128, 128], P('ry')
Inputs may be any that keep to these rules, and one draw needn't show every extreme that they name: `signs`: each entry is -1 or 1. `indices`: local row numbers; repeats allowed; entries of dead slots are ignored. `counts`: some device has all 256 slots live.
All inputs are finite; a program needn't handle non-finite values.
Results may differ from a plain program's by a relative error of at most 0.00011.
Values sent between devices are 32-bit elements; how exact they have to be, the bound alone decides.
A program may use at most 64 MiB of HBM per device.

v0:
```python
import jax
import jax.numpy as jnp
from jax import lax
from jax.sharding import PartitionSpec as P

BLK = 128


def partner_2(value, axis, distance):
    return lax.ppermute(value, axis, [(i, i ^ 1 << distance) for i in range(lax.axis_size(axis))])


def hadamard(order):
    idx = jnp.arange(order, dtype=jnp.int32)
    both = jnp.bitwise_and(idx[:, None], idx[None, :])
    parity = jnp.zeros((order, order), jnp.int32)
    for shift in range(order.bit_length() - 1):
        parity = parity + jnp.bitwise_and(jnp.right_shift(both, shift), 1)
    return (1 - 2 * (parity % 2)).astype(jnp.float32)


def local(matrix, signs, indices, counts):
    rows, width = matrix.shape
    panel = width // 2
    size_x = lax.axis_size("rx")
    size_y = lax.axis_size("ry")
    signed = matrix * signs[:, None].astype(jnp.float32)
    blocks = signed.reshape(rows // BLK, BLK, width)
    mixed = jnp.einsum(
        "ij,bjc->bic", hadamard(BLK), blocks, precision=lax.Precision.HIGHEST
    ).reshape(rows, width)
    for shift in range(size_y.bit_length() - 1):
        partner = partner_2(mixed, "ry", shift)
        upper = jnp.bitwise_and(jnp.right_shift(lax.axis_index("ry"), shift), 1) == 1
        mixed = jnp.where(upper, partner - mixed, mixed + partner)
    for shift in range(size_x.bit_length() - 1):
        partner = partner_2(mixed, "rx", shift)
        upper = jnp.bitwise_and(jnp.right_shift(lax.axis_index("rx"), shift), 1) == 1
        mixed = jnp.where(upper, partner - mixed, mixed + partner)
    mixed = mixed * (1.0 / (size_x * size_y * BLK) ** 0.5)
    slots = indices.shape[0]
    live = jnp.arange(slots, dtype=jnp.int32) < counts[0]
    picked = jnp.take(mixed, indices, axis=0)
    sketch = jnp.where(live[:, None], picked, jnp.float32(0.0))
    factor = 1.0 / (size_x * size_y * slots)
    owner = lax.axis_index("ry")
    left_start = owner // 2 * panel
    right_start = owner % 2 * panel
    piece = lax.all_gather(sketch, "ry", axis=0, tiled=True)
    left = lax.dynamic_slice_in_dim(piece, left_start, panel, 1)
    right = lax.dynamic_slice_in_dim(piece, right_start, panel, 1)
    partial_block = jnp.dot(left.T, right, precision=lax.Precision.HIGHEST)
    block = lax.psum(partial_block, "rx")
    gram_blocks = (block * factor)[None]
    return (sketch, gram_blocks)


def solution(mesh):
    in_specs = (P(("rx", "ry"), None), P(("rx", "ry")), P(("rx", "ry")), P(("rx", "ry")))
    out_specs = (P(("rx", "ry"), None), P("ry", None, None))
    return jax.shard_map(local, mesh=mesh, in_specs=in_specs, out_specs=out_specs, check_vma=False)
```

profile of v0, /device:TPU:1, one launch (start us, length us, event | category | flops | bytes accessed | tf_op | source)
XLA Modules:
  0.0 760.1 jit_solution(2804836046712218144)
XLA Ops:
  7.2 0.0 all-gather.2.cloned.1.call-start
  7.2 0.7 convert_element_type.7
  7.9 2.6 broadcast_multiply_fusion
  10.5 5.5 fusion.8
  16.0 2.0 collective-permute-start
  18.1 90.1 %collective-permute-done = f32[4096,256]{1,0:T(8,128)} collective-permute-done((f32[4096,256]{1,0:T(8,128)}, f32[4096,256]{1,0:T(8,128)}, u32[]{:S(2)}, u32[]{:S(2)}) %collective-permute-start) | collective-permute-done | bytes 4194336 | tf_op jit(solution)/shard_map/ppermute | solution.py:10
  108.2 6.0 add_select_fusion.5
  114.1 3.2 collective-permute-start.1
  117.3 89.4 %collective-permute-done.1 = f32[4096,256]{1,0:T(8,128)} collective-permute-done((f32[4096,256]{1,0:T(8,128)}, f32[4096,256]{1,0:T(8,128)}, u32[]{:S(2)}, u32[]{:S(2)}) %collective-permute-start.1) | collective-permute-done | bytes 4194336 | tf_op jit(solution)/shard_map/ppermute | solution.py:10
  206.7 6.0 add_select_fusion.4
  212.7 2.4 collective-permute-start.2
  215.1 7.1 collective-permute-done.2
  222.2 6.0 add_select_fusion.3
  228.2 1.8 collective-permute-start.3
  230.0 91.0 %collective-permute-done.3 = f32[4096,256]{1,0:T(8,128)} collective-permute-done((f32[4096,256]{1,0:T(8,128)}, f32[4096,256]{1,0:T(8,128)}, u32[]{:S(2)}, u32[]{:S(2)}) %collective-permute-start.3) | collective-permute-done | bytes 4194336 | tf_op jit(solution)/shard_map/ppermute | solution.py:10
  321.0 6.0 add_select_fusion.2
  326.9 3.1 collective-permute-start.4
  330.1 90.0 %collective-permute-done.4 = f32[4096,256]{1,0:T(8,128)} collective-permute-done((f32[4096,256]{1,0:T(8,128)}, f32[4096,256]{1,0:T(8,128)}, u32[]{:S(2)}, u32[]{:S(2)}) %collective-permute-start.4) | collective-permute-done | bytes 4194336 | tf_op jit(solution)/shard_map/ppermute | solution.py:10
  420.1 6.0 add_select_fusion.1
  426.0 1.3 collective-permute-start.5
  427.3 0.0 copy-start
  427.3 89.3 %collective-permute-done.5 = f32[4096,256]{1,0:T(8,128)} collective-permute-done((f32[4096,256]{1,0:T(8,128)}, f32[4096,256]{1,0:T(8,128)}, u32[]{:S(2)}, u32[]{:S(2)}) %collective-permute-start.5) | collective-permute-done | bytes 4194336 | tf_op jit(solution)/shard_map/ppermute | solution.py:10
  516.6 6.0 add_select_fusion
  522.5 2.9 collective-permute-start.6
  526.1 0.0 copy-done
  526.2 87.5 %collective-permute-done.6 = f32[4096,256]{1,0:T(8,128)} collective-permute-done((f32[4096,256]{1,0:T(8,128)}, f32[4096,256]{1,0:T(8,128)}, u32[]{:S(2)}, u32[]{:S(2)}) %collective-permute-start.6) | collective-permute-done | bytes 4194336 | tf_op jit(solution)/shard_map/ppermute | solution.py:10
  613.7 6.0 select_multiply_fusion
  619.6 3.2 gather_fusion
  622.8 0.8 select_select_fusion
  623.6 0.0 all-gather.2.cloned.1.call-update
  623.7 0.0 all-reduce.2.cloned.1.call-start
  623.7 27.3 %all-gather.2.cloned.1.call-done = f32[1024,256]{1,0:T(8,128)} async-done(((f32[256,256]{1,0:T(8,128)}), f32[1024,256]{1,0:T(8,128)}) %all-gather.2.cloned.1.call-update) | async-done | bytes 1048592 | tf_op jit(solution)/shard_map/all_gather | solution.py:49
  651.0 2.9 fusion
  653.9 0.0 all-reduce.2.cloned.1.call-update
  653.9 97.9 %all-reduce.2.cloned.1.call-done = f32[128,128]{1,0:T(8,128)} async-done(((f32[128,128]{1,0:T(8,128)}), f32[128,128]{1,0:T(8,128)}) %all-reduce.2.cloned.1.call-update) | async-done | bytes 65552 | tf_op jit(solution)/shard_map/psum | solution.py:53
  751.8 1.5 multiply_bitcast_fusion
  (3 shorter events, 0.0 us)
Async XLA Ops:
  7.2 643.8 %all-gather.2.cloned.1.call-start = ((), (), s32[]{:S(2)}) async-start(), calls=%async_computation | async-start | bytes 1310720 | tf_op jit(solution)/shard_map/all_gather | solution.py:49
  16.0 92.1 %collective-permute-start = (f32[4096,256]{1,0:T(8,128)}, f32[4096,256]{1,0:T(8,128)}, u32[]{:S(2)}, u32[]{:S(2)}) collective-permute-start(f32[4096,256]{1,0:T(8,128)} %bitcast.4), channel_id=1, source_target_pairs={{0,1},{1,0},{2,3},{3,2},{4,5},{5,4},{6,7},{7,6},{8,9},{9,8},{10,11... | collective-permute-start | bytes 12582920 | tf_op jit(solution)/shard_map/ppermute | solution.py:10
  114.1 92.6 %collective-permute-start.1 = (f32[4096,256]{1,0:T(8,128)}, f32[4096,256]{1,0:T(8,128)}, u32[]{:S(2)}, u32[]{:S(2)}) collective-permute-start(f32[4096,256]{1,0:T(8,128)} %add_select_fusion.5), channel_id=1, source_target_pairs={{0,2},{1,3},{2,0},{3,1},{4,6},{5,7},{6,4},{7,5},{8,10},{9,11},{10,... | collective-permute-start | bytes 12582920 | tf_op jit(solution)/shard_map/ppermute | solution.py:10
  212.7 9.6 %collective-permute-start.2 = (f32[4096,256]{1,0:T(8,128)}, f32[4096,256]{1,0:T(8,128)}, u32[]{:S(2)}, u32[]{:S(2)}) collective-permute-start(f32[4096,256]{1,0:T(8,128)} %add_select_fusion.4), channel_id=1, source_target_pairs={{0,4},{4,0},{8,12},{12,8},{16,20},{20,16},{24,28},{28,24},{32,36},... | collective-permute-start | bytes 12582920 | tf_op jit(solution)/shard_map/ppermute | solution.py:10
  228.2 92.8 %collective-permute-start.3 = (f32[4096,256]{1,0:T(8,128)}, f32[4096,256]{1,0:T(8,128)}, u32[]{:S(2)}, u32[]{:S(2)}) collective-permute-start(f32[4096,256]{1,0:T(8,128)} %add_select_fusion.3), channel_id=1, source_target_pairs={{0,8},{4,12},{8,0},{12,4},{16,24},{20,28},{24,16},{28,20},{32,40},... | collective-permute-start | bytes 12582920 | tf_op jit(solution)/shard_map/ppermute | solution.py:10
  326.9 93.1 %collective-permute-start.4 = (f32[4096,256]{1,0:T(8,128)}, f32[4096,256]{1,0:T(8,128)}, u32[]{:S(2)}, u32[]{:S(2)}) collective-permute-start(f32[4096,256]{1,0:T(8,128)} %add_select_fusion.2), channel_id=1, source_target_pairs={{0,16},{4,20},{8,24},{12,28},{16,0},{20,4},{24,8},{28,12},{32,48},... | collective-permute-start | bytes 12582920 | tf_op jit(solution)/shard_map/ppermute | solution.py:10
  426.0 90.6 %collective-permute-start.5 = (f32[4096,256]{1,0:T(8,128)}, f32[4096,256]{1,0:T(8,128)}, u32[]{:S(2)}, u32[]{:S(2)}) collective-permute-start(f32[4096,256]{1,0:T(8,128)} %add_select_fusion.1), channel_id=1, source_target_pairs={{0,32},{4,36},{8,40},{12,44},{16,48},{20,52},{24,56},{28,60},{32,0... | collective-permute-start | bytes 12582920 | tf_op jit(solution)/shard_map/ppermute | solution.py:10
  427.3 98.8 %copy-start = (s32[256]{0:T(256)S(1)}, s32[256]{0:T(256)}, u32[]{:S(2)}) copy-start(s32[256]{0:T(256)} %param.6) | copy-start | bytes 3076
  522.5 91.1 %collective-permute-start.6 = (f32[4096,256]{1,0:T(8,128)}, f32[4096,256]{1,0:T(8,128)}, u32[]{:S(2)}, u32[]{:S(2)}) collective-permute-start(f32[4096,256]{1,0:T(8,128)} %add_select_fusion), channel_id=1, source_target_pairs={{0,64},{4,68},{8,72},{12,76},{16,80},{20,84},{24,88},{28,92},{32,9... | collective-permute-start | bytes 12582920 | tf_op jit(solution)/shard_map/ppermute | solution.py:10
  623.7 128.1 %all-reduce.2.cloned.1.call-start = ((), (), s32[]{:S(2)}) async-start(), calls=%async_computation.1 | async-start | bytes 131072 | tf_op jit(solution)/shard_map/psum | solution.py:53
Sparse Core Ops, SparseCore 0:
  623.8 27.1 all-gather.1
  654.8 96.8 all-reduce.1
where the time goes:
time: 760 us
  waiting for transfers between devices  670 us (88%)
  other arithmetic  47.3 us (6%)
  starting transfers between devices  16.9 us (2%)
  between operations  14.8 us (2%)
  matrix products  8.36 us (1%)
    ppermute x7, waiting for transfers between devices, partner_2(): lax.ppermute(value, axis, [(i, i ^ 1 << distance) for i in range(lax.axis...  544 us
    psum x1, waiting for transfers between devices, local(): block = lax.psum(partial_block, 'rx')  97.9 us
    select_n x6, other arithmetic, local(): mixed = jnp.where(upper, partner - mixed, mixed + partner)  35.7 us
    all_gather x1, waiting for transfers between devices, local(): piece = lax.all_gather(sketch, 'ry', axis=0, tiled=True)  27.3 us
    ppermute x7, starting transfers between devices, partner_2(): lax.ppermute(value, axis, [(i, i ^ 1 << distance) for i in range(lax.axis...  16.8 us
  transfers between devices with their start and end apart: 9, of which 9 were waited for; matrix products, arithmetic and copies ran while one was open for 0% of the time, Pallas kernels for 0%

commit v1 on v0

v1 whole, which is shorter than its diff:
```python
import functools

import jax
import jax.numpy as jnp
from jax import lax
from jax.experimental import pallas as pl
from jax.experimental.pallas import tpu as pltpu
from jax.sharding import PartitionSpec as P

MESH = pl.DeviceIdType.MESH
BLK = 128
HALF = 64
PARTS = (
    (0, "y", "x", "z"),
    (0, "x", "z", "y"),
    (1, "y", "z", "x"),
    (1, "z", "x", "y"),
)


def coords():
    rx = lax.axis_index("rx")
    return {"y": rx // 8, "z": (rx // 2) % 4, "c": rx % 2, "x": lax.axis_index("ry")}


def device(at):
    return ((at["y"] * 4 + at["z"]) * 2 + at["c"], at["x"])


def moved(at, **to):
    return device({**at, **to})


def sign4(a, b):
    odd = (a % 2) * (b % 2) + (a // 2) * (b // 2)
    return (1 - 2 * (odd % 2)).astype(jnp.float32)


def hadamard(n):
    both = lax.broadcasted_iota(jnp.int32, (n, n), 0) & lax.broadcasted_iota(jnp.int32, (n, n), 1)
    both = both ^ (both >> 4)
    both = both ^ (both >> 2)
    both = both ^ (both >> 1)
    return (1 - 2 * (both & 1)).astype(jnp.float32)


def kernel(
    x_hbm, sg, idx, cnt, sk_out, gr_out,
    xm, xo, so, had, a, b, c, d0, d1, d2, d3, e, f, g, h,
    tile, ly, lz, pzy, pxy, pxz, szy, sxy, sxz, gp, rb, co, ob,
    loc_sem, core_s, core_r, st_s, st_r, ix_s, ix_r, sm_sem, rs_s, rs_r, ag_s, ag_r,
):
    me = coords()
    done = (d0, d1, d2, d3)
    lane = lax.broadcasted_iota(jnp.int32, (1, 128), 1) < HALF
    other = moved(me, c=1 - me["c"])

    def local(panel):
        cols = pl.ds(panel * 128, 128)
        return pltpu.make_async_copy(x_hbm.at[:, cols], xm.at[:, cols], loc_sem.at[panel])

    def remote(src, dst, send, recv, to):
        return pltpu.make_async_remote_copy(
            src_ref=src, dst_ref=dst, send_sem=send, recv_sem=recv, device_id=to, device_id_type=MESH
        )

    for panel in range(2):
        local(panel).start()

    barrier = pltpu.get_barrier_semaphore()

    def greet(o, _):
        to = moved(me, y=(me["y"] + o // 16) % 4, z=(me["z"] + (o // 4) % 4) % 4, x=(me["x"] + o % 4) % 4)
        pl.semaphore_signal(barrier, inc=1, device_id=to, device_id_type=MESH)
        return 0

    pl.semaphore_signal(barrier, inc=1, device_id=other, device_id_type=MESH)
    lax.fori_loop(1, 64, greet, 0)

    had[...] = hadamard(BLK)
    rows = idx[...]
    tile[...] = jnp.zeros_like(tile)
    tile[pl.ds(0, 1), :] = rows[0:1, :]
    tile[pl.ds(1, 1), :] = rows[1:2, :] ^ 2048
    pl.semaphore_wait(barrier, 64)

    def core(i):
        if i == 2:
            return remote(sg, so, core_s.at[i], core_r.at[i], other)
        cols = pl.ds(i * 128, 128)
        return remote(x_hbm.at[:, cols], xo.at[:, cols], core_s.at[i], core_r.at[i], other)

    core(2).start()
    core(0).start()
    core(1).start()

    def line(buf, axis, n, dist):
        at = (me[axis] + dist) % 4
        mine = pl.ds(pl.multiple_of(me[axis] * 8, 8), 8)
        i = n * 3 + dist - 1
        return remote(tile, buf.at[mine, :], ix_s.at[i], ix_r.at[i], moved(me, **{axis: at}))

    def plane(src, buf, axis, n, dist):
        at = (me[axis] + dist) % 4
        mine = pl.ds(pl.multiple_of(me[axis] * 32, 32), 32)
        i = 6 + n * 3 + dist - 1
        return remote(src, buf.at[mine, :], ix_s.at[i], ix_r.at[i], moved(me, **{axis: at}))

    lines = ((ly, "y", 0), (lz, "z", 1))
    planes = ((ly, pzy, "z", 0), (ly, pxy, "x", 1), (lz, pxz, "x", 2))
    for buf, axis, n in lines:
        for dist in (1, 2, 3):
            line(buf, axis, n, dist).start()
        buf[pl.ds(pl.multiple_of(me[axis] * 8, 8), 8), :] = tile[...]

    def exchange(stage, part, dist):
        axis = PARTS[part][1 if stage < 2 else stage]
        at = (me[axis] + dist) % 4
        src, dst = ((a, b), (c, None), (e, f), (g, h))[stage]
        size = 128 if stage == 3 else 512
        i = (stage * 4 + part) * 3 + dist - 1
        mine = pl.ds(pl.multiple_of(me[axis] * size, size), size)
        return remote(
            src.at[part, pl.ds(pl.multiple_of(at * size, size), size), :],
            done[part].at[mine, :] if stage == 1 else dst.at[part, mine, :],
            st_s.at[i], st_r.at[i], moved(me, **{axis: at}),
        )

    def send(stage, part):
        for dist in (1, 2, 3):
            exchange(stage, part, dist).start()

    def arrive(stage, part):
        for dist in (1, 2, 3):
            exchange(stage, part, dist).wait_recv()

    def start_part(panel):
        sign = (1 - 2 * me["c"]).astype(jnp.float32)
        cols = pl.ds(panel * 128, 128)

        def block(at):
            place = pl.ds(pl.multiple_of(at * BLK, BLK), BLK)
            s0 = sg[pl.ds(at, 1), :].astype(jnp.float32) * sign
            s1 = so[pl.ds(at, 1), :].astype(jnp.float32)
            hm = had[...]
            left = jnp.concatenate([hm * s0, hm * s1], axis=1).astype(jnp.bfloat16)
            both = jnp.concatenate([xm[place, cols], xo[place, cols]], axis=0)
            hi = both.astype(jnp.bfloat16)
            lo = (both - hi.astype(jnp.float32)).astype(jnp.bfloat16)
            out = jnp.dot(left, jnp.concatenate([hi, lo], axis=1), preferred_element_type=jnp.float32)
            return out[:, :128] + out[:, 128:]

        def pair(i, _):
            lo, hi = block(i), block(i + 16)
            place = pl.ds(pl.multiple_of(i * BLK, BLK), BLK)
            a[2 * panel, place, :] = jnp.where(lane, lo, pltpu.roll(hi, HALF, 1))
            a[2 * panel + 1, place, :] = jnp.where(lane, pltpu.roll(lo, HALF, 1), hi)
            return 0

        lax.fori_loop(0, 16, pair, 0)

    def own(axis, size):
        return pl.ds(pl.multiple_of(me[axis] * size, size), size)

    def transform(part):
        def step(i, _):
            v = [b[part, pl.ds(pl.multiple_of(q * 512 + i * 32, 32), 32), :] for q in range(4)]
            s, t, u, w = v[0] + v[1], v[0] - v[1], v[2] + v[3], v[2] - v[3]
            for q, out in enumerate((s + u, t + w, s - u, t - w)):
                c[part, pl.ds(pl.multiple_of(q * 512 + i * 32, 32), 32), :] = out
            return 0

        lax.fori_loop(0, 16, step, 0)

    def whole(part):
        axis = PARTS[part][1]
        b[part, own(axis, 512), :] = a[part, own(axis, 512), :]
        arrive(0, part)
        transform(part)
        send(1, part)
        done[part][own(axis, 512), :] = c[part, own(axis, 512), :]

    def gather(part, m, dst):
        table, swap = ((sxz, False), (szy, False), (sxz, True), (sxy, False))[part]
        rows = done[part]

        def some(i, _):
            l, k0 = i // 8, (i % 8) * 16
            row = ((l * 4 + m) if swap else (m * 4 + l)) * 8
            for u in range(16):
                lo = rows[pl.ds(table[row, k0 + u], 1), :]
                hi = rows[pl.ds(table[row + 1, k0 + u], 1), :]
                dst[part, pl.ds(m * 512 + i * 16 + u, 1), :] = jnp.where(lane, lo, hi)
            return 0

        lax.fori_loop(0, 32, some, 0)

    def pruned(part):
        axis = PARTS[part][2]
        arrive(1, part)

        def turn(i, _):
            v = done[part][pl.ds(pl.multiple_of(i * 64, 64), 64), :]
            done[part][pl.ds(pl.multiple_of(2048 + i * 64, 64), 64), :] = pltpu.roll(v, HALF, 1)
            return 0

        lax.fori_loop(0, 32, turn, 0)
        for dist in (1, 2, 3):
            gather(part, (me[axis] + dist) % 4, e)
            exchange(2, part, dist).start()
        gather(part, me[axis], f)

    def add_up(part, src, size, axis):
        signs = [sign4(me[axis], jnp.int32(q)) for q in range(4)]

        def at(start, count):
            total = src[part, pl.ds(start, count), :]
            for q in range(1, 4):
                total = total + signs[q] * src[part, pl.ds(pl.multiple_of(q * size + start, 8), count), :]
            return total

        return at

    def last(part):
        axis = PARTS[part][3]
        arrive(2, part)
        sums = add_up(part, f, 512, PARTS[part][2])

        def step(i, _):
            start = pl.multiple_of(i * 32, 32)
            g[part, pl.ds(start, 32), :] = sums(start, 32)
            return 0

        lax.fori_loop(0, 16, step, 0)
        send(3, part)
        h[part, own(axis, 128), :] = g[part, own(axis, 128), :]

    def final(part):
        arrive(3, part)
        return add_up(part, h, 128, PARTS[part][3])(0, 128)

    local(0).wait()
    core(2).wait_recv()
    core(0).wait_recv()
    start_part(0)
    send(0, 0)
    send(0, 1)
    local(1).wait()
    core(1).wait_recv()
    start_part(1)
    send(0, 3)
    send(0, 2)

    for buf, axis, n in lines:
        for dist in (1, 2, 3):
            line(buf, axis, n, dist).wait_recv()
    for src, buf, axis, n in planes:
        for dist in (1, 2, 3):
            plane(src, buf, axis, n, dist).start()
        buf[pl.ds(pl.multiple_of(me[axis] * 32, 32), 32), :] = src[...]

    whole(1)
    whole(0)
    whole(3)
    for i, (src, buf, axis, n) in enumerate(planes):
        for dist in (1, 2, 3):
            plane(src, buf, axis, n, dist).wait_recv()
        pltpu.make_async_copy(buf, (szy, sxy, sxz)[i], sm_sem.at[i]).start()
    whole(2)
    for i, (src, buf, axis, n) in enumerate(planes):
        pltpu.make_async_copy(buf, (szy, sxy, sxz)[i], sm_sem.at[i]).wait()

    pruned(1)
    pruned(3)
    pruned(0)
    last(1)
    last(3)
    pruned(2)
    last(0)
    last(2)

    scale = 1.0 / (128 * BLK) ** 0.5
    slot = lax.broadcasted_iota(jnp.int32, (128, 1), 0)
    count = cnt[0]
    for panel in range(2):
        p1 = final(2 * panel + 1)
        p0 = final(2 * panel)
        cols = pl.ds(panel * 128, 128)
        lo = jnp.where(lane, p0, pltpu.roll(p1, HALF, 1)) * scale
        hi = jnp.where(lane, pltpu.roll(p0, HALF, 1), p1) * scale
        sk_out[pl.ds(0, 128), cols] = jnp.where(slot < count, lo, 0.0)
        sk_out[pl.ds(128, 128), cols] = jnp.where(slot + 128 < count, hi, 0.0)

    sk = sk_out[...]
    hi = sk.astype(jnp.bfloat16)
    lo = (sk - hi.astype(jnp.float32)).astype(jnp.bfloat16)

    def dot_t(p, q):
        return lax.dot_general(p, q, (((0,), (0,)), ((), ())), preferred_element_type=jnp.float32)

    gram = dot_t(hi, hi) + dot_t(hi, lo) + dot_t(lo, hi)
    for i in range(4):
        gp[pl.ds(i * 128, 128), :] = gram[i // 2 * 128 : i // 2 * 128 + 128, i % 2 * 128 : i % 2 * 128 + 128]

    here = me["y"] * 4 + me["z"]

    def piece(o):
        to = {"y": (me["y"] + o // 16) % 4, "z": (me["z"] + (o // 4) % 4) % 4, "x": (me["x"] + o % 4) % 4}
        src = pl.multiple_of(to["x"] * 128 + (to["y"] * 4 + to["z"]) * 8, 8)
        dst = pl.multiple_of((here * 4 + me["x"]) * 8, 8)
        return remote(gp.at[pl.ds(src, 8), :], rb.at[pl.ds(dst, 8), :], rs_s.at[o], rs_r.at[o], moved(me, **to))

    lax.fori_loop(1, 64, lambda o, _: (piece(o).start(), 0)[1], 0)
    rb[pl.ds(pl.multiple_of((here * 4 + me["x"]) * 8, 8), 8), :] = gp[
        pl.ds(pl.multiple_of(me["x"] * 128 + here * 8, 8), 8), :
    ]
    lax.fori_loop(1, 64, lambda o, _: (piece(o).wait_recv(), 0)[1], 0)
    co[pl.ds(0, 8), :] = rb[...].reshape(64, 8, 128).sum(0)
    swap = remote(co.at[pl.ds(0, 8), :], co.at[pl.ds(8, 8), :], core_s.at[3], core_r.at[3], other)
    swap.start()
    swap.wait_recv()
    mine = pl.ds(pl.multiple_of(here * 8, 8), 8)
    ob[mine, :] = (co[pl.ds(0, 8), :] + co[pl.ds(8, 8), :]) * (1.0 / (128 * 256))

    def share(o):
        to = {"y": (me["y"] + o // 4) % 4, "z": (me["z"] + o % 4) % 4}
        return remote(ob.at[mine, :], ob.at[mine, :], ag_s.at[o], ag_r.at[o], moved(me, **to))

    lax.fori_loop(1, 16, lambda o, _: (share(o).start(), 0)[1], 0)
    lax.fori_loop(1, 16, lambda o, _: (share(o).wait_recv(), 0)[1], 0)
    gr_out[...] = ob[...]

    lax.fori_loop(1, 16, lambda o, _: (share(o).wait_send(), 0)[1], 0)
    swap.wait_send()
    lax.fori_loop(1, 64, lambda o, _: (piece(o).wait_send(), 0)[1], 0)
    for i in range(3):
        core(i).wait_send()
    for dist in (1, 2, 3):
        for buf, axis, n in lines:
            line(buf, axis, n, dist).wait_send()
        for src, buf, axis, n in planes:
            plane(src, buf, axis, n, dist).wait_send()
        for stage in range(4):
            for part in range(4):
                exchange(stage, part, dist).wait_send()


def local(matrix, signs, indices, counts):
    f32, i32 = jnp.float32, jnp.int32
    vmem, smem, dma = pltpu.VMEM, pltpu.SMEM, pltpu.SemaphoreType.DMA
    in_vmem = pl.BlockSpec(memory_space=vmem)
    sketch, gram = pl.pallas_call(
        kernel,
        name="sketch_gram",
        out_shape=(jax.ShapeDtypeStruct((256, 256), f32), jax.ShapeDtypeStruct((128, 128), f32)),
        in_specs=[pl.BlockSpec(memory_space=pl.ANY), in_vmem, in_vmem, pl.BlockSpec(memory_space=smem)],
        out_specs=(in_vmem, in_vmem),
        scratch_shapes=[
            vmem((4096, 256), f32), vmem((4096, 256), f32), vmem((32, 128), i32), vmem((128, 128), f32),
            vmem((4, 2048, 128), f32), vmem((4, 2048, 128), f32), vmem((4, 2048, 128), f32),
            *[vmem((4096, 128), f32)] * 4, vmem((4, 2048, 128), f32), vmem((4, 2048, 128), f32),
            vmem((4, 512, 128), f32), vmem((4, 512, 128), f32),
            vmem((8, 128), i32), vmem((32, 128), i32), vmem((32, 128), i32),
            vmem((128, 128), i32), vmem((128, 128), i32), vmem((128, 128), i32),
            smem((128, 128), i32), smem((128, 128), i32), smem((128, 128), i32),
            vmem((512, 128), f32), vmem((512, 128), f32), vmem((16, 128), f32), vmem((128, 128), f32),
            dma((2,)), dma((4,)), dma((4,)), dma((48,)), dma((48,)), dma((15,)), dma((15,)), dma((3,)),
            dma((64,)), dma((64,)), dma((16,)), dma((16,)),
        ],
        compiler_params=pltpu.CompilerParams(
            collective_id=0, has_side_effects=True, vmem_limit_bytes=56 * 2**20
        ),
    )(matrix, signs.reshape(32, 128), indices.reshape(2, 128), counts)
    return sketch, gram[None]


def solution(mesh):
    in_specs = (P(("rx", "ry"), None), P(("rx", "ry")), P(("rx", "ry")), P(("rx", "ry")))
    out_specs = (P(("rx", "ry"), None), P("ry", None, None))
    return jax.shard_map(local, mesh=mesh, in_specs=in_specs, out_specs=out_specs, check_vma=False)
```

time: 760 us -> 130 us (0.17)
  waiting for transfers between devices: 670 us -> 0 us
  Pallas kernels: 0 us -> 125 us
  other arithmetic: 47.3 us -> 0 us
  starting transfers between devices: 16.9 us -> 0 us
  between operations: 14.8 us -> 1.29 us
  matrix products: 8.36 us -> 0 us
    ppermute x7 -> x0, waiting for transfers between devices: 544 us -> none  [partner_2(): lax.ppermute(value, axis, [(i, i ^ 1 << distance) for i in range(lax.axis...]
    pallas_call x0 -> x1, Pallas kernels: none -> 125 us  [local(): pl.pallas_call(kernel, name='sketch_gram', out_shape=(jax.ShapeDtypeStruc...]
    psum x1 -> x0, waiting for transfers between devices: 97.9 us -> none  [local(): block = lax.psum(partial_block, 'rx')]
    select_n x8 -> x0, other arithmetic: 36.6 us -> none  [the longest x6 35.7 us: local(): mixed = jnp.where(upper, partner - mixed, mixed + partner)]
    all_gather x1 -> x0, waiting for transfers between devices: 27.3 us -> none  [local(): piece = lax.all_gather(sketch, 'ry', axis=0, tiled=True)]
    ppermute x7 -> x0, starting transfers between devices: 16.8 us -> none  [partner_2(): lax.ppermute(value, axis, [(i, i ^ 1 << distance) for i in range(lax.axis...]
    mul x2 -> x0, other arithmetic: 8.54 us -> none  [the longest x1 5.96 us: local(): mixed = mixed * (1.0 / (size_x * size_y * BLK) ** 0.5)]
    dot_general x2 -> x0, matrix products: 8.36 us -> none  [the longest x1 5.51 us: local(): jnp.einsum('ij,bjc->bic', hadamard(BLK), blocks, precision=lax.Precision....]
  transfers between devices with their start and end apart: 9 -> 0, of which waited for: 9 -> 0; matrix products, arithmetic and copies ran while one was open for 0% -> 0% of each run, Pallas kernels for 0% -> 0%
where the time goes in v1:
time: 130 us
  Pallas kernels  125 us (96%)
  local copies, waits for them, and re-layouts  3.14 us (2%)
    pallas_call x1, Pallas kernels, local(): pl.pallas_call(kernel, name='sketch_gram', out_shape=(jax.ShapeDtypeStruc...  125 us
    unnamed x2, local copies, waits for them, and re-layouts  3.14 us

profile of v1, /device:TPU:1, one launch (start us, length us, event | category | flops | bytes accessed | tf_op | source)
XLA Modules:
  0.0 129.6 jit_solution(10855270789978352716)
XLA Ops:
  1.3 125.2 %sketch_gram.1 = (f32[256,256]{1,0:T(8,128)}, f32[128,128]{1,0:T(8,128)}) custom-call(f32[4096,256]{1,0:T(8,128)} %x_hbm.1, s32[32,128]{1,0:T(8,128)} %bitcast.4, s32[2,128]{1,0:T(2,128)} %bitcast.5, s32[1]{0:T(128)S(6)} %copy.8.cnt), custom_call_target="tpu_custom_call" | custom-call | tf_op jit(solution)/shard_map/sketch_gram/pallas_call | solution.py:352
  126.4 1.7 %copy.9 = f32[256,256]{1,0:T(8,128)} copy(f32[256,256]{1,0:T(8,128)} %get-tuple-element.8) | data formatting | bytes 524288
  128.1 1.5 %copy.10 = f32[1,128,128]{2,1,0:T(8,128)} copy(f32[1,128,128]{2,1,0:T(8,128)} %bitcast.3) | data formatting | bytes 131072

commit v2 on v1

v2 whole, which is shorter than its diff:
```python
import functools

import jax
import jax.numpy as jnp
from jax import lax
from jax.experimental import pallas as pl
from jax.experimental.pallas import tpu as pltpu
from jax.sharding import PartitionSpec as P

MESH = pl.DeviceIdType.MESH
BLK = 128
HALF = 64
PARTS = (("y", "x", "z"), ("x", "z", "y"), ("y", "z", "x"), ("z", "x", "y"))


def coords():
    rx = lax.axis_index("rx")
    return {"y": rx // 8, "z": (rx // 2) % 4, "c": rx % 2, "x": lax.axis_index("ry")}


def device(at):
    return ((at["y"] * 4 + at["z"]) * 2 + at["c"], at["x"])


def moved(at, **to):
    return device({**at, **to})


def sign4(a, b):
    odd = (a % 2) * (b % 2) + (a // 2) * (b // 2)
    return (1 - 2 * (odd % 2)).astype(jnp.float32)


def hadamard(n):
    both = lax.broadcasted_iota(jnp.int32, (n, n), 0) & lax.broadcasted_iota(jnp.int32, (n, n), 1)
    both = both ^ (both >> 4)
    both = both ^ (both >> 2)
    both = both ^ (both >> 1)
    return (1 - 2 * (both & 1)).astype(jnp.float32)


def kernel(
    x_hbm, sg, idx, cnt, sk_out, gr_out,
    xm, xo, so, had, ry, ro, sy, syo, cy, dy, r, a, b, c, d1, d3, e, f, g, h,
    tile, ly, lz, pzy, pxy, pxz, szy, sxy, sxz, gp, rb, co, ob,
    loc_sem, core_s, core_r, y_s, y_r, st_s, st_r, ix_s, ix_r, sm_sem, rs_s, rs_r, ag_s, ag_r,
):
    me = coords()
    done = {1: d1, 3: d3}
    lane = lax.broadcasted_iota(jnp.int32, (1, 128), 1) < HALF
    other = moved(me, c=1 - me["c"])

    def rows(start, size):
        return pl.ds(pl.multiple_of(start, 8), size)

    def remote(src, dst, send, recv, to):
        return pltpu.make_async_remote_copy(
            src_ref=src, dst_ref=dst, send_sem=send, recv_sem=recv, device_id=to, device_id_type=MESH
        )

    load = pltpu.make_async_copy(x_hbm.at[:, pl.ds(128, 128)], xm, loc_sem.at[0])
    keep = pltpu.make_async_copy(
        x_hbm.at[rows(me["y"] * 1024, 1024), pl.ds(0, 128)], ry.at[me["y"]], loc_sem.at[1]
    )
    load.start()
    keep.start()

    barrier = pltpu.get_barrier_semaphore()

    def greet(o, _):
        to = moved(me, y=(me["y"] + o // 16) % 4, z=(me["z"] + (o // 4) % 4) % 4, x=(me["x"] + o % 4) % 4)
        pl.semaphore_signal(barrier, inc=1, device_id=to, device_id_type=MESH)
        return 0

    pl.semaphore_signal(barrier, inc=1, device_id=other, device_id_type=MESH)
    lax.fori_loop(1, 64, greet, 0)

    had[...] = hadamard(BLK)
    slots = idx[...]
    tile[...] = jnp.zeros_like(tile)
    tile[pl.ds(0, 1), :] = slots[0:1, :]
    tile[pl.ds(1, 1), :] = slots[1:2, :] ^ 2048
    tile[pl.ds(2, 1), :] = slots[1:2, :]
    pl.semaphore_wait(barrier, 64)

    def core(i):
        if i == 8:
            return remote(sg, so, core_s.at[i], core_r.at[i], other)
        place = pl.ds(i % 2 * 2048 + i // 2 * 512, 512)
        return remote(x_hbm.at[place, pl.ds(128, 128)], xo.at[place, :], core_s.at[i], core_r.at[i], other)

    def out_y(k, dist):
        at = (me["y"] + dist) % 4
        i = k * 3 + dist - 1
        if k == 4:
            src, dst = sg.at[rows(at * 8, 8), :], sy.at[rows(me["y"] * 8, 8), :]
        else:
            src = x_hbm.at[rows(at * 1024 + k * 256, 256), pl.ds(0, 128)]
            dst = ry.at[me["y"], pl.ds(k * 256, 256), :]
        return remote(src, dst, y_s.at[i], y_r.at[i], moved(me, y=at))

    def back_y(k, dist):
        at = (me["y"] + dist) % 4
        i = 15 + k * 3 + dist - 1
        return remote(
            cy.at[at, pl.ds(k * 256, 256), :], dy.at[rows(me["y"] * 1024 + k * 256, 256), :],
            y_s.at[i], y_r.at[i], moved(me, y=at),
        )

    def core_y(k):
        i = 9 + k
        if k == 4:
            return remote(sy, syo, core_s.at[i], core_r.at[i], other)
        place = pl.ds(k * 256, 256)
        return remote(ry.at[:, place, :], ro.at[:, place, :], core_s.at[i], core_r.at[i], other)

    core(8).start()
    for i in range(2):
        core(i).start()
    for dist in (1, 2, 3):
        out_y(4, dist).start()
        out_y(0, dist).start()
    for i in range(2, 8):
        core(i).start()
    for k in range(1, 4):
        for dist in (1, 2, 3):
            out_y(k, dist).start()

    def line(buf, axis, n, dist):
        at = (me[axis] + dist) % 4
        i = n * 3 + dist - 1
        return remote(tile, buf.at[rows(me[axis] * 8, 8), :], ix_s.at[i], ix_r.at[i], moved(me, **{axis: at}))

    def plane(src, buf, axis, n, dist):
        at = (me[axis] + dist) % 4
        i = 6 + n * 3 + dist - 1
        return remote(src, buf.at[rows(me[axis] * 32, 32), :], ix_s.at[i], ix_r.at[i], moved(me, **{axis: at}))

    lines = ((ly, "y", 0), (lz, "z", 1))
    planes = ((ly, pzy, "z", 0), (ly, pxy, "x", 1), (lz, pxz, "x", 2))
    for buf, axis, n in lines:
        for dist in (1, 2, 3):
            line(buf, axis, n, dist).start()
        buf[rows(me[axis] * 8, 8), :] = tile[...]

    def exchange(stage, part, dist):
        axis = PARTS[part][max(stage - 1, 0)]
        at = (me[axis] + dist) % 4
        size = 128 if stage == 3 else 512
        i = (stage * 4 + part) * 3 + dist - 1
        src = (a, c, e, g)[stage].at[part // 2 if stage < 2 else part, rows(at * size, size), :]
        mine = rows(me[axis] * size, size)
        if stage == 1:
            dst = done[part].at[mine, :]
        else:
            dst = (b, None, f, h)[stage].at[part // 2 if stage < 2 else part, mine, :]
        return remote(src, dst, st_s.at[i], st_r.at[i], moved(me, **{axis: at}))

    def send(stage, part):
        for dist in (1, 2, 3):
            exchange(stage, part, dist).start()

    def arrive(stage, part):
        for dist in (1, 2, 3):
            exchange(stage, part, dist).wait_recv()

    sign = (1 - 2 * me["c"]).astype(jnp.float32)

    def mixed(s0, s1, x0, x1):
        hm = had[...]
        left = jnp.concatenate(
            [hm * (s0.astype(jnp.float32) * sign), hm * s1.astype(jnp.float32)], axis=1
        ).astype(jnp.bfloat16)
        both = jnp.concatenate([x0, x1], axis=0)
        hi = both.astype(jnp.bfloat16)
        lo = (both - hi.astype(jnp.float32)).astype(jnp.bfloat16)
        out = jnp.dot(left, jnp.concatenate([hi, lo], axis=1), preferred_element_type=jnp.float32)
        return out[:, :128] + out[:, 128:]

    def panel1(j):
        def block(at):
            place = rows(at * BLK, BLK)
            return mixed(sg[pl.ds(at, 1), :], so[pl.ds(at, 1), :], xm[place, :], xo[place, :])

        def pair(i, _):
            lo, hi = block(i), block(i + 16)
            place = rows(i * BLK, BLK)
            a[0, place, :] = jnp.where(lane, lo, pltpu.roll(hi, HALF, 1))
            a[1, place, :] = jnp.where(lane, pltpu.roll(lo, HALF, 1), hi)
            return 0

        lax.fori_loop(4 * j, 4 * j + 4, pair, 0)

    def four(v):
        s, t, u, w = v[0] + v[1], v[0] - v[1], v[2] + v[3], v[2] - v[3]
        return s + u, t + w, s - u, t - w

    def panel0(k):
        def step(n, _):
            at = k * 2 + n
            place = rows(at * BLK, BLK)
            v = [
                mixed(sy[pl.ds(q * 8 + at, 1), :], syo[pl.ds(q * 8 + at, 1), :], ry[q, place, :], ro[q, place, :])
                for q in range(4)
            ]
            for q, out in enumerate(four(v)):
                cy[q, place, :] = out
            return 0

        lax.fori_loop(0, 2, step, 0)
        for dist in (1, 2, 3):
            back_y(k, dist).start()
        dy[rows(me["y"] * 1024 + k * 256, 256), :] = cy[me["y"], pl.ds(k * 256, 256), :]

    def across(k):
        for dist in (1, 2, 3):
            out_y(k, dist).wait_recv()
        core_y(k).start()

    def own(axis, size):
        return rows(me[axis] * size, size)

    def whole(part):
        n, axis = part // 2, PARTS[part][0]
        b[n, own(axis, 512), :] = a[n, own(axis, 512), :]
        arrive(0, part)

        def step(i, _):
            for q, out in enumerate(four([b[n, rows(q * 512 + i * 32, 32), :] for q in range(4)])):
                c[n, rows(q * 512 + i * 32, 32), :] = out
            return 0

        lax.fori_loop(0, 16, step, 0)
        send(1, part)
        done[part][own(axis, 512), :] = c[n, own(axis, 512), :]

    def gather(part, m, dst):
        table, src = {1: szy, 3: sxy}[part], done[part]

        def some(i, _):
            row, k0 = (m * 4 + i // 2) * 8, (i % 2) * 64
            for u in range(64):
                lo = src[pl.ds(table[row, k0 + u], 1), :]
                hi = src[pl.ds(table[row + 1, k0 + u], 1), :]
                dst[part, pl.ds(m * 512 + i * 64 + u, 1), :] = jnp.where(lane, lo, hi)
            return 0

        lax.fori_loop(0, 8, some, 0)

    def pruned(part):
        axis = PARTS[part][1]
        arrive(1, part)

        def turn(i, _):
            done[part][rows(2048 + i * 64, 64), :] = pltpu.roll(done[part][rows(i * 64, 64), :], HALF, 1)
            return 0

        lax.fori_loop(0, 32, turn, 0)
        for dist in (1, 2, 3):
            gather(part, (me[axis] + dist) % 4, e)
            exchange(2, part, dist).start()
        gather(part, me[axis], f)

    def cells(xs, zs):
        def cell(n, _):
            x = (me["x"] + (xs[0] + n if len(xs) > 1 else xs[0])) % 4
            z = (me["z"] + (zs[0] + n if len(zs) > 1 else zs[0])) % 4
            row = (x * 4 + z) * 8

            def some(i, _):
                for u in range(32):
                    r[pl.ds(i * 32 + u, 1), :] = dy[pl.ds(sxz[row, i * 32 + u], 1), :]
                    r[pl.ds(128 + i * 32 + u, 1), :] = dy[pl.ds(sxz[row + 2, i * 32 + u], 1), :]
                return 0

            lax.fori_loop(0, 4, some, 0)
            lo, hi = r[pl.ds(0, 128), :], r[pl.ds(128, 128), :]
            e[0, rows(x * 512 + z * 128, 128), :] = jnp.where(lane, lo, pltpu.roll(hi, HALF, 1))
            e[2, rows(z * 512 + x * 128, 128), :] = jnp.where(lane, pltpu.roll(lo, HALF, 1), hi)
            return 0

        lax.fori_loop(0, max(len(xs), len(zs)), cell, 0)

    def pruned_y():
        for k in range(4):
            for dist in (1, 2, 3):
                back_y(k, dist).wait_recv()
        for dist in (1, 2, 3):
            cells((dist,), range(dist, 5))
            exchange(2, 0, dist).start()
            cells(range(dist + 1, 5), (dist,))
            exchange(2, 2, dist).start()
        cells((4,), (4,))
        for part in (0, 2):
            f[part, own(PARTS[part][1], 512), :] = e[part, own(PARTS[part][1], 512), :]

    def add_up(part, src, size, axis):
        signs = [sign4(me[axis], jnp.int32(q)) for q in range(4)]

        def at(start, count):
            total = src[part, pl.ds(start, count), :]
            for q in range(1, 4):
                total = total + signs[q] * src[part, rows(q * size + start, count), :]
            return total

        return at

    def last(part):
        axis = PARTS[part][2]
        arrive(2, part)
        sums = add_up(part, f, 512, PARTS[part][1])

        def step(i, _):
            start = pl.multiple_of(i * 32, 32)
            g[part, pl.ds(start, 32), :] = sums(start, 32)
            return 0

        lax.fori_loop(0, 16, step, 0)
        send(3, part)
        h[part, own(axis, 128), :] = g[part, own(axis, 128), :]

    def final(part):
        arrive(3, part)
        return add_up(part, h, 128, PARTS[part][2])(0, 128)

    load.wait()
    core(8).wait_recv()
    for j in range(4):
        core(2 * j).wait_recv()
        core(2 * j + 1).wait_recv()
        panel1(j)
        for part in (1, 3):
            axis = PARTS[part][0]

            @pl.when(me[axis] != j)
            def _():
                exchange(0, part, (j - me[axis] + 4) % 4).start()

    keep.wait()
    for dist in (1, 2, 3):
        out_y(4, dist).wait_recv()
    sy[own("y", 8), :] = sg[own("y", 8), :]
    core_y(4).start()
    across(0)
    for buf, axis, n in lines:
        for dist in (1, 2, 3):
            line(buf, axis, n, dist).wait_recv()
    for src, buf, axis, n in planes:
        for dist in (1, 2, 3):
            plane(src, buf, axis, n, dist).start()
        buf[rows(me[axis] * 32, 32), :] = src[...]
    core_y(4).wait_recv()
    core_y(0).wait_recv()
    panel0(0)
    across(1)
    core_y(1).wait_recv()
    panel0(1)
    across(2)
    whole(1)
    core_y(2).wait_recv()
    panel0(2)
    whole(3)
    across(3)
    core_y(3).wait_recv()
    panel0(3)
    for i, (src, buf, axis, n) in enumerate(planes):
        for dist in (1, 2, 3):
            plane(src, buf, axis, n, dist).wait_recv()
        pltpu.make_async_copy(buf, (szy, sxy, sxz)[i], sm_sem.at[i]).start()
    for i, (src, buf, axis, n) in enumerate(planes):
        pltpu.make_async_copy(buf, (szy, sxy, sxz)[i], sm_sem.at[i]).wait()

    pruned(1)
    pruned(3)
    pruned_y()
    last(1)
    last(3)
    last(0)
    last(2)

    scale = 1.0 / (128 * BLK) ** 0.5
    slot = lax.broadcasted_iota(jnp.int32, (128, 1), 0)
    count = cnt[0]
    for panel in (1, 0):
        p1 = final(3 if panel else 2)
        p0 = final(1 if panel else 0)
        cols = pl.ds(panel * 128, 128)
        lo = jnp.where(lane, p0, pltpu.roll(p1, HALF, 1)) * scale
        hi = jnp.where(lane, pltpu.roll(p0, HALF, 1), p1) * scale
        sk_out[pl.ds(0, 128), cols] = jnp.where(slot < count, lo, 0.0)
        sk_out[pl.ds(128, 128), cols] = jnp.where(slot + 128 < count, hi, 0.0)

    sk = sk_out[...]
    hi = sk.astype(jnp.bfloat16)
    lo = (sk - hi.astype(jnp.float32)).astype(jnp.bfloat16)

    def dot_t(p, q):
        return lax.dot_general(p, q, (((0,), (0,)), ((), ())), preferred_element_type=jnp.float32)

    gram = dot_t(hi, hi) + dot_t(hi, lo) + dot_t(lo, hi)
    for i in range(4):
        gp[pl.ds(i * 128, 128), :] = gram[i // 2 * 128 : i // 2 * 128 + 128, i % 2 * 128 : i % 2 * 128 + 128]

    here = me["y"] * 4 + me["z"]

    def piece(o):
        to = {"y": (me["y"] + o // 16) % 4, "z": (me["z"] + (o // 4) % 4) % 4, "x": (me["x"] + o % 4) % 4}
        src = pl.multiple_of(to["x"] * 128 + (to["y"] * 4 + to["z"]) * 8, 8)
        dst = pl.multiple_of((here * 4 + me["x"]) * 8, 8)
        return remote(gp.at[pl.ds(src, 8), :], rb.at[pl.ds(dst, 8), :], rs_s.at[o], rs_r.at[o], moved(me, **to))

    lax.fori_loop(1, 64, lambda o, _: (piece(o).start(), 0)[1], 0)
    rb[pl.ds(pl.multiple_of((here * 4 + me["x"]) * 8, 8), 8), :] = gp[
        pl.ds(pl.multiple_of(me["x"] * 128 + here * 8, 8), 8), :
    ]
    lax.fori_loop(1, 64, lambda o, _: (piece(o).wait_recv(), 0)[1], 0)
    co[pl.ds(0, 8), :] = rb[...].reshape(64, 8, 128).sum(0)
    swap = remote(co.at[pl.ds(0, 8), :], co.at[pl.ds(8, 8), :], core_s.at[14], core_r.at[14], other)
    swap.start()
    swap.wait_recv()
    mine = pl.ds(pl.multiple_of(here * 8, 8), 8)
    ob[mine, :] = (co[pl.ds(0, 8), :] + co[pl.ds(8, 8), :]) * (1.0 / (128 * 256))

    def share(o):
        to = {"y": (me["y"] + o // 4) % 4, "z": (me["z"] + o % 4) % 4}
        return remote(ob.at[mine, :], ob.at[mine, :], ag_s.at[o], ag_r.at[o], moved(me, **to))

    lax.fori_loop(1, 16, lambda o, _: (share(o).start(), 0)[1], 0)
    lax.fori_loop(1, 16, lambda o, _: (share(o).wait_recv(), 0)[1], 0)
    gr_out[...] = ob[...]

    lax.fori_loop(1, 16, lambda o, _: (share(o).wait_send(), 0)[1], 0)
    swap.wait_send()
    lax.fori_loop(1, 64, lambda o, _: (piece(o).wait_send(), 0)[1], 0)
    for i in range(9):
        core(i).wait_send()
    for k in range(5):
        core_y(k).wait_send()
    for dist in (1, 2, 3):
        for buf, axis, n in lines:
            line(buf, axis, n, dist).wait_send()
        for src, buf, axis, n in planes:
            plane(src, buf, axis, n, dist).wait_send()
        for k in range(5):
            out_y(k, dist).wait_send()
        for k in range(4):
            back_y(k, dist).wait_send()
        for stage in range(4):
            for part in (1, 3) if stage < 2 else range(4):
                exchange(stage, part, dist).wait_send()


def local(matrix, signs, indices, counts):
    f32, i32 = jnp.float32, jnp.int32
    vmem, smem, dma = pltpu.VMEM, pltpu.SMEM, pltpu.SemaphoreType.DMA
    in_vmem = pl.BlockSpec(memory_space=vmem)
    sketch, gram = pl.pallas_call(
        kernel,
        name="sketch_gram",
        out_shape=(jax.ShapeDtypeStruct((256, 256), f32), jax.ShapeDtypeStruct((128, 128), f32)),
        in_specs=[pl.BlockSpec(memory_space=pl.ANY), in_vmem, in_vmem, pl.BlockSpec(memory_space=smem)],
        out_specs=(in_vmem, in_vmem),
        scratch_shapes=[
            vmem((4096, 128), f32), vmem((4096, 128), f32), vmem((32, 128), i32), vmem((128, 128), f32),
            vmem((4, 1024, 128), f32), vmem((4, 1024, 128), f32), vmem((32, 128), i32), vmem((32, 128), i32),
            vmem((4, 1024, 128), f32), vmem((4096, 128), f32), vmem((256, 128), f32),
            vmem((2, 2048, 128), f32), vmem((2, 2048, 128), f32), vmem((2, 2048, 128), f32),
            vmem((4096, 128), f32), vmem((4096, 128), f32),
            vmem((4, 2048, 128), f32), vmem((4, 2048, 128), f32),
            vmem((4, 512, 128), f32), vmem((4, 512, 128), f32),
            vmem((8, 128), i32), vmem((32, 128), i32), vmem((32, 128), i32),
            vmem((128, 128), i32), vmem((128, 128), i32), vmem((128, 128), i32),
            smem((128, 128), i32), smem((128, 128), i32), smem((128, 128), i32),
            vmem((512, 128), f32), vmem((512, 128), f32), vmem((16, 128), f32), vmem((128, 128), f32),
            dma((2,)), dma((15,)), dma((15,)), dma((27,)), dma((27,)), dma((48,)), dma((48,)),
            dma((15,)), dma((15,)), dma((3,)), dma((64,)), dma((64,)), dma((16,)), dma((16,)),
        ],
        compiler_params=pltpu.CompilerParams(
            collective_id=0, has_side_effects=True, vmem_limit_bytes=56 * 2**20
        ),
    )(matrix, signs.reshape(32, 128), indices.reshape(2, 128), counts)
    return sketch, gram[None]


def solution(mesh):
    in_specs = (P(("rx", "ry"), None), P(("rx", "ry")), P(("rx", "ry")), P(("rx", "ry")))
    out_specs = (P(("rx", "ry"), None), P("ry", None, None))
    return jax.shard_map(local, mesh=mesh, in_specs=in_specs, out_specs=out_specs, check_vma=False)
```

time: 130 us -> 122 us (0.938)
  Pallas kernels: 125 us -> 117 us
    pallas_call x1, Pallas kernels: 125 us -> 117 us  [local(): pl.pallas_call(kernel, name='sketch_gram', out_shape=(jax.ShapeDtypeStruc...]
where the time goes in v2:
time: 122 us
  Pallas kernels  117 us (96%)
  local copies, waits for them, and re-layouts  3.14 us (3%)
  between operations  1.29 us (1%)
    pallas_call x1, Pallas kernels, local(): pl.pallas_call(kernel, name='sketch_gram', out_shape=(jax.ShapeDtypeStruc...  117 us
    unnamed x2, local copies, waits for them, and re-layouts  3.14 us

profile of v2, /device:TPU:1, one launch (start us, length us, event | category | flops | bytes accessed | tf_op | source)
XLA Modules:
  0.0 121.8 jit_solution(16799710073946631277)
XLA Ops:
  1.3 117.3 %sketch_gram.1 = (f32[256,256]{1,0:T(8,128)}, f32[128,128]{1,0:T(8,128)}) custom-call(f32[4096,256]{1,0:T(8,128)} %x_hbm.1, s32[32,128]{1,0:T(8,128)} %bitcast.4, s32[2,128]{1,0:T(2,128)} %bitcast.5, s32[1]{0:T(128)S(6)} %copy.8.cnt), custom_call_target="tpu_custom_call" | custom-call | tf_op jit(solution)/shard_map/sketch_gram/pallas_call | solution.py:457
  118.6 1.7 %copy.9 = f32[256,256]{1,0:T(8,128)} copy(f32[256,256]{1,0:T(8,128)} %get-tuple-element.8) | data formatting | bytes 524288
  120.3 1.5 %copy.10 = f32[1,128,128]{2,1,0:T(8,128)} copy(f32[1,128,128]{2,1,0:T(8,128)} %bitcast.3) | data formatting | bytes 131072

commit v3 on v2

--- a/solution.py
+++ b/solution.py
@@ -114,6 +114,23 @@
         place = pl.ds(k * 256, 256)
         return remote(ry.at[:, place, :], ro.at[:, place, :], core_s.at[i], core_r.at[i], other)
 
+    def line(buf, axis, n, dist):
+        at = (me[axis] + dist) % 4
+        i = n * 3 + dist - 1
+        return remote(tile, buf.at[rows(me[axis] * 8, 8), :], ix_s.at[i], ix_r.at[i], moved(me, **{axis: at}))
+
+    def plane(src, buf, axis, n, dist):
+        at = (me[axis] + dist) % 4
+        i = 6 + n * 3 + dist - 1
+        return remote(src, buf.at[rows(me[axis] * 32, 32), :], ix_s.at[i], ix_r.at[i], moved(me, **{axis: at}))
+
+    lines = ((ly, "y", 0), (lz, "z", 1))
+    planes = ((ly, pzy, "z", 0), (ly, pxy, "x", 1), (lz, pxz, "x", 2))
+    for buf, axis, n in lines:
+        for dist in (1, 2, 3):
+            line(buf, axis, n, dist).start()
+        buf[rows(me[axis] * 8, 8), :] = tile[...]
+
     core(8).start()
     for i in range(2):
         core(i).start()
@@ -125,23 +142,6 @@
     for k in range(1, 4):
         for dist in (1, 2, 3):
             out_y(k, dist).start()
-
-    def line(buf, axis, n, dist):
-        at = (me[axis] + dist) % 4
-        i = n * 3 + dist - 1
-        return remote(tile, buf.at[rows(me[axis] * 8, 8), :], ix_s.at[i], ix_r.at[i], moved(me, **{axis: at}))
-
-    def plane(src, buf, axis, n, dist):
-        at = (me[axis] + dist) % 4
-        i = 6 + n * 3 + dist - 1
-        return remote(src, buf.at[rows(me[axis] * 32, 32), :], ix_s.at[i], ix_r.at[i], moved(me, **{axis: at}))
-
-    lines = ((ly, "y", 0), (lz, "z", 1))
-    planes = ((ly, pzy, "z", 0), (ly, pxy, "x", 1), (lz, pxz, "x", 2))
-    for buf, axis, n in lines:
-        for dist in (1, 2, 3):
-            line(buf, axis, n, dist).start()
-        buf[rows(me[axis] * 8, 8), :] = tile[...]
 
     def exchange(stage, part, dist):
         axis = PARTS[part][max(stage - 1, 0)]

time: 122 us -> 115 us (0.943)
  Pallas kernels: 117 us -> 110 us
    pallas_call x1, Pallas kernels: 117 us -> 110 us  [local(): pl.pallas_call(kernel, name='sketch_gram', out_shape=(jax.ShapeDtypeStruc...]
where the time goes in v3:
time: 115 us
  Pallas kernels  110 us (96%)
  local copies, waits for them, and re-layouts  3.14 us (3%)
  between operations  1.29 us (1%)
    pallas_call x1, Pallas kernels, local(): pl.pallas_call(kernel, name='sketch_gram', out_shape=(jax.ShapeDtypeStruc...  110 us
    unnamed x2, local copies, waits for them, and re-layouts  3.14 us

profile of v3, /device:TPU:1, one launch (start us, length us, event | category | flops | bytes accessed | tf_op | source)
XLA Modules:
  0.0 114.6 jit_solution(5577733671263943275)
XLA Ops:
  1.3 110.1 %sketch_gram.1 = (f32[256,256]{1,0:T(8,128)}, f32[128,128]{1,0:T(8,128)}) custom-call(f32[4096,256]{1,0:T(8,128)} %x_hbm.1, s32[32,128]{1,0:T(8,128)} %bitcast.4, s32[2,128]{1,0:T(2,128)} %bitcast.5, s32[1]{0:T(128)S(6)} %copy.8.cnt), custom_call_target="tpu_custom_call" | custom-call | tf_op jit(solution)/shard_map/sketch_gram/pallas_call | solution.py:457
  111.4 1.7 %copy.9 = f32[256,256]{1,0:T(8,128)} copy(f32[256,256]{1,0:T(8,128)} %get-tuple-element.8) | data formatting | bytes 524288
  113.1 1.5 %copy.10 = f32[1,128,128]{2,1,0:T(8,128)} copy(f32[1,128,128]{2,1,0:T(8,128)} %bitcast.3) | data formatting | bytes 131072

commit v4 on v3

--- a/solution.py
+++ b/solution.py
@@ -51,7 +51,7 @@
     other = moved(me, c=1 - me["c"])
 
     def rows(start, size):
-        return pl.ds(pl.multiple_of(start, 8), size)
+        return pl.ds(pl.multiple_of(start, 1024 if size % 1024 == 0 else 8), size)
 
     def remote(src, dst, send, recv, to):
         return pltpu.make_async_remote_copy(
@@ -76,11 +76,10 @@
     lax.fori_loop(1, 64, greet, 0)
 
     had[...] = hadamard(BLK)
-    slots = idx[...]
     tile[...] = jnp.zeros_like(tile)
-    tile[pl.ds(0, 1), :] = slots[0:1, :]
-    tile[pl.ds(1, 1), :] = slots[1:2, :] ^ 2048
-    tile[pl.ds(2, 1), :] = slots[1:2, :]
+    tile[pl.ds(0, 128)] = idx[pl.ds(0, 128)]
+    tile[pl.ds(128, 128)] = idx[pl.ds(128, 128)] ^ 2048
+    tile[pl.ds(256, 128)] = idx[pl.ds(128, 128)]
     pl.semaphore_wait(barrier, 64)
 
     def core(i):
@@ -117,19 +116,19 @@
     def line(buf, axis, n, dist):
         at = (me[axis] + dist) % 4
         i = n * 3 + dist - 1
-        return remote(tile, buf.at[rows(me[axis] * 8, 8), :], ix_s.at[i], ix_r.at[i], moved(me, **{axis: at}))
+        return remote(tile, buf.at[rows(me[axis] * 1024, 1024)], ix_s.at[i], ix_r.at[i], moved(me, **{axis: at}))
 
     def plane(src, buf, axis, n, dist):
         at = (me[axis] + dist) % 4
         i = 6 + n * 3 + dist - 1
-        return remote(src, buf.at[rows(me[axis] * 32, 32), :], ix_s.at[i], ix_r.at[i], moved(me, **{axis: at}))
+        return remote(src, buf.at[rows(me[axis] * 4096, 4096)], ix_s.at[i], ix_r.at[i], moved(me, **{axis: at}))
 
     lines = ((ly, "y", 0), (lz, "z", 1))
     planes = ((ly, pzy, "z", 0), (ly, pxy, "x", 1), (lz, pxz, "x", 2))
     for buf, axis, n in lines:
         for dist in (1, 2, 3):
             line(buf, axis, n, dist).start()
-        buf[rows(me[axis] * 8, 8), :] = tile[...]
+        buf[rows(me[axis] * 1024, 1024)] = tile[...]
 
     core(8).start()
     for i in range(2):
@@ -238,10 +237,10 @@
         table, src = {1: szy, 3: sxy}[part], done[part]
 
         def some(i, _):
-            row, k0 = (m * 4 + i // 2) * 8, (i % 2) * 64
+            base = (m * 4 + i // 2) * 1024 + (i % 2) * 64
             for u in range(64):
-                lo = src[pl.ds(table[row, k0 + u], 1), :]
-                hi = src[pl.ds(table[row + 1, k0 + u], 1), :]
+                lo = src[pl.ds(table[base + u], 1), :]
+                hi = src[pl.ds(table[base + 128 + u], 1), :]
                 dst[part, pl.ds(m * 512 + i * 64 + u, 1), :] = jnp.where(lane, lo, hi)
             return 0
 
@@ -265,12 +264,13 @@
         def cell(n, _):
             x = (me["x"] + (xs[0] + n if len(xs) > 1 else xs[0])) % 4
             z = (me["z"] + (zs[0] + n if len(zs) > 1 else zs[0])) % 4
-            row = (x * 4 + z) * 8
+            base = (x * 4 + z) * 1024
+            table = sxz
 
             def some(i, _):
                 for u in range(32):
-                    r[pl.ds(i * 32 + u, 1), :] = dy[pl.ds(sxz[row, i * 32 + u], 1), :]
-                    r[pl.ds(128 + i * 32 + u, 1), :] = dy[pl.ds(sxz[row + 2, i * 32 + u], 1), :]
+                    r[pl.ds(i * 32 + u, 1), :] = dy[pl.ds(table[base + i * 32 + u], 1), :]
+                    r[pl.ds(128 + i * 32 + u, 1), :] = dy[pl.ds(table[base + 256 + i * 32 + u], 1), :]
                 return 0
 
             lax.fori_loop(0, 4, some, 0)
@@ -348,72 +348,100 @@
     for src, buf, axis, n in planes:
         for dist in (1, 2, 3):
             plane(src, buf, axis, n, dist).start()
-        buf[rows(me[axis] * 32, 32), :] = src[...]
+        buf[rows(me[axis] * 4096, 4096)] = src[...]
     core_y(4).wait_recv()
     core_y(0).wait_recv()
     panel0(0)
     across(1)
     core_y(1).wait_recv()
     panel0(1)
+    whole(1)
+    whole(3)
     across(2)
-    whole(1)
     core_y(2).wait_recv()
     panel0(2)
-    whole(3)
+
+    def to_smem(i):
+        return pltpu.make_async_copy(planes[i][1], (szy, sxy, sxz)[i], sm_sem.at[i])
+
+    for i, (src, buf, axis, n) in enumerate(planes):
+        for dist in (1, 2, 3):
+            plane(src, buf, axis, n, dist).wait_recv()
+        to_smem(i).start()
     across(3)
     core_y(3).wait_recv()
     panel0(3)
-    for i, (src, buf, axis, n) in enumerate(planes):
-        for dist in (1, 2, 3):
-            plane(src, buf, axis, n, dist).wait_recv()
-        pltpu.make_async_copy(buf, (szy, sxy, sxz)[i], sm_sem.at[i]).start()
-    for i, (src, buf, axis, n) in enumerate(planes):
-        pltpu.make_async_copy(buf, (szy, sxy, sxz)[i], sm_sem.at[i]).wait()
-
+    for i in range(3):
+        to_smem(i).wait()
     pruned(1)
     pruned(3)
     pruned_y()
-    last(1)
-    last(3)
-    last(0)
-    last(2)
-
     scale = 1.0 / (128 * BLK) ** 0.5
     slot = lax.broadcasted_iota(jnp.int32, (128, 1), 0)
     count = cnt[0]
-    for panel in (1, 0):
-        p1 = final(3 if panel else 2)
-        p0 = final(1 if panel else 0)
+
+    def finish(panel, lower, upper):
+        p0, p1 = final(lower), final(upper)
         cols = pl.ds(panel * 128, 128)
         lo = jnp.where(lane, p0, pltpu.roll(p1, HALF, 1)) * scale
         hi = jnp.where(lane, pltpu.roll(p0, HALF, 1), p1) * scale
         sk_out[pl.ds(0, 128), cols] = jnp.where(slot < count, lo, 0.0)
         sk_out[pl.ds(128, 128), cols] = jnp.where(slot + 128 < count, hi, 0.0)
-
-    sk = sk_out[...]
-    hi = sk.astype(jnp.bfloat16)
-    lo = (sk - hi.astype(jnp.float32)).astype(jnp.bfloat16)
-
-    def dot_t(p, q):
-        return lax.dot_general(p, q, (((0,), (0,)), ((), ())), preferred_element_type=jnp.float32)
-
-    gram = dot_t(hi, hi) + dot_t(hi, lo) + dot_t(lo, hi)
-    for i in range(4):
-        gp[pl.ds(i * 128, 128), :] = gram[i // 2 * 128 : i // 2 * 128 + 128, i % 2 * 128 : i % 2 * 128 + 128]
+        sk = sk_out[:, cols]
+        hi = sk.astype(jnp.bfloat16)
+        return hi, (sk - hi.astype(jnp.float32)).astype(jnp.bfloat16)
 
     here = me["y"] * 4 + me["z"]
 
-    def piece(o):
-        to = {"y": (me["y"] + o // 16) % 4, "z": (me["z"] + (o // 4) % 4) % 4, "x": (me["x"] + o % 4) % 4}
-        src = pl.multiple_of(to["x"] * 128 + (to["y"] * 4 + to["z"]) * 8, 8)
-        dst = pl.multiple_of((here * 4 + me["x"]) * 8, 8)
-        return remote(gp.at[pl.ds(src, 8), :], rb.at[pl.ds(dst, 8), :], rs_s.at[o], rs_r.at[o], moved(me, **to))
-
-    lax.fori_loop(1, 64, lambda o, _: (piece(o).start(), 0)[1], 0)
-    rb[pl.ds(pl.multiple_of((here * 4 + me["x"]) * 8, 8), 8), :] = gp[
-        pl.ds(pl.multiple_of(me["x"] * 128 + here * 8, 8), 8), :
-    ]
-    lax.fori_loop(1, 64, lambda o, _: (piece(o).wait_recv(), 0)[1], 0)
+    def gram(n, p, q):
+        def dot(u, v):
+            return lax.dot_general(u, v, (((0,), (0,)), ((), ())), preferred_element_type=jnp.float32)
+
+        gp[pl.ds(n * 128, 128), :] = dot(p[0], q[0]) + dot(p[0], q[1]) + dot(p[1], q[0])
+
+    def piece(dx, o):
+        to = {"y": (me["y"] + o // 4) % 4, "z": (me["z"] + o % 4) % 4, "x": (me["x"] + dx) % 4}
+        src = to["x"] * 128 + (to["y"] * 4 + to["z"]) * 8
+        dst = (here * 4 + me["x"]) * 8
+        n = dx * 16 + o
+        return remote(gp.at[rows(src, 8), :], rb.at[rows(dst, 8), :], rs_s.at[n], rs_r.at[n], moved(me, **to))
+
+    def scatter(n):
+        dx = (n - me["x"] + 4) % 4
+
+        def step(o, _):
+            piece(dx, o).start()
+            return 0
+
+        lax.fori_loop(1, 16, step, 0)
+
+        @pl.when(dx != 0)
+        def _():
+            piece(dx, 0).start()
+
+    def each_piece(act):
+        def step(n, _):
+            act(piece(n // 16, n % 16))
+            return 0
+
+        lax.fori_loop(1, 64, step, 0)
+
+    last(1)
+    last(3)
+    sk1 = finish(1, 1, 3)
+    gram(3, sk1, sk1)
+    scatter(3)
+    last(0)
+    last(2)
+    sk0 = finish(0, 0, 2)
+    gram(0, sk0, sk0)
+    scatter(0)
+    gram(1, sk0, sk1)
+    scatter(1)
+    gram(2, sk1, sk0)
+    scatter(2)
+    rb[rows((here * 4 + me["x"]) * 8, 8), :] = gp[rows(me["x"] * 128 + here * 8, 8), :]
+    each_piece(lambda p: p.wait_recv())
     co[pl.ds(0, 8), :] = rb[...].reshape(64, 8, 128).sum(0)
     swap = remote(co.at[pl.ds(0, 8), :], co.at[pl.ds(8, 8), :], core_s.at[14], core_r.at[14], other)
     swap.start()
@@ -431,7 +459,7 @@
 
     lax.fori_loop(1, 16, lambda o, _: (share(o).wait_send(), 0)[1], 0)
     swap.wait_send()
-    lax.fori_loop(1, 64, lambda o, _: (piece(o).wait_send(), 0)[1], 0)
+    each_piece(lambda p: p.wait_send())
     for i in range(9):
         core(i).wait_send()
     for k in range(5):
@@ -448,6 +476,14 @@
         for stage in range(4):
             for part in (1, 3) if stage < 2 else range(4):
                 exchange(stage, part, dist).wait_send()
+
+
+def hand_on(a, b, to_a, to_b, sem):
+    both = pltpu.make_async_copy(a, to_a, sem.at[0]), pltpu.make_async_copy(b, to_b, sem.at[1])
+    for copy in both:
+        copy.start()
+    for copy in both:
+        copy.wait()
 
 
 def local(matrix, signs, indices, counts):
@@ -468,9 +504,9 @@
             vmem((4096, 128), f32), vmem((4096, 128), f32),
             vmem((4, 2048, 128), f32), vmem((4, 2048, 128), f32),
             vmem((4, 512, 128), f32), vmem((4, 512, 128), f32),
-            vmem((8, 128), i32), vmem((32, 128), i32), vmem((32, 128), i32),
-            vmem((128, 128), i32), vmem((128, 128), i32), vmem((128, 128), i32),
-            smem((128, 128), i32), smem((128, 128), i32), smem((128, 128), i32),
+            vmem((1024,), i32), vmem((4096,), i32), vmem((4096,), i32),
+            vmem((16384,), i32), vmem((16384,), i32), vmem((16384,), i32),
+            smem((16384,), i32), smem((16384,), i32), smem((16384,), i32),
             vmem((512, 128), f32), vmem((512, 128), f32), vmem((16, 128), f32), vmem((128, 128), f32),
             dma((2,)), dma((15,)), dma((15,)), dma((27,)), dma((27,)), dma((48,)), dma((48,)),
             dma((15,)), dma((15,)), dma((3,)), dma((64,)), dma((64,)), dma((16,)), dma((16,)),
@@ -478,7 +514,16 @@
         compiler_params=pltpu.CompilerParams(
             collective_id=0, has_side_effects=True, vmem_limit_bytes=56 * 2**20
         ),
-    )(matrix, signs.reshape(32, 128), indices.reshape(2, 128), counts)
+    )(matrix, signs.reshape(32, 128), indices, counts)
+    anywhere = pl.BlockSpec(memory_space=pl.ANY)
+    sketch, gram = pl.pallas_call(
+        hand_on,
+        name="hand_on",
+        out_shape=(jax.ShapeDtypeStruct((256, 256), f32), jax.ShapeDtypeStruct((128, 128), f32)),
+        in_specs=[anywhere] * 2,
+        out_specs=(anywhere,) * 2,
+        scratch_shapes=[dma((2,))],
+    )(sketch, gram)
     return sketch, gram[None]
 
 

time: 115 us -> 122 us (1.061)
  Pallas kernels: 110 us -> 120 us
  local copies, waits for them, and re-layouts: 3.14 us -> 0 us
    pallas_call x0 -> x1, Pallas kernels: none -> 11 us  [local(): pl.pallas_call(hand_on, name='hand_on', out_shape=(jax.ShapeDtypeStruct((...]
    unnamed x2 -> x0, local copies, waits for them, and re-layouts: 3.14 us -> none
where the time goes in v4:
time: 122 us; the launch traced here: 121 us
  Pallas kernels  120 us (98%)
  between operations  1.28 us (1%)
    pallas_call x1, Pallas kernels, local(): pl.pallas_call(kernel, name='sketch_gram', out_shape=(jax.ShapeDtypeStruc...  109 us
    pallas_call x1, Pallas kernels, local(): pl.pallas_call(hand_on, name='hand_on', out_shape=(jax.ShapeDtypeStruct((...  11 us

profile of v4, /device:TPU:1, one launch (start us, length us, event | category | flops | bytes accessed | tf_op | source)
XLA Modules:
  0.0 121.5 jit_solution(11419904640730083841)
XLA Ops:
  1.3 109.1 %sketch_gram.1 = (f32[256,256]{1,0:T(8,128)}, f32[128,128]{1,0:T(8,128)}) custom-call(f32[4096,256]{1,0:T(8,128)} %x_hbm.1, s32[32,128]{1,0:T(8,128)} %bitcast.2, s32[256]{0:T(256)} %idx.1, s32[1]{0:T(128)S(6)} %copy.6.cnt), custom_call_target="tpu_custom_call" | custom-call | tf_op jit(solution)/shard_map/sketch_gram/pallas_call | solution.py:493
  110.4 11.0 %hand_on.1 = (f32[256,256]{1,0:T(8,128)}, f32[128,128]{1,0:T(8,128)}) custom-call(f32[256,256]{1,0:T(8,128)} %get-tuple-element.6.a, f32[128,128]{1,0:T(8,128)} %get-tuple-element.7.b), custom_call_target="tpu_custom_call" | custom-call | tf_op jit(solution)/shard_map/hand_on/pallas_call | solution.py:519

commit v5 on v4

--- a/solution.py
+++ b/solution.py
@@ -67,20 +67,18 @@
 
     barrier = pltpu.get_barrier_semaphore()
 
-    def greet(o, _):
-        to = moved(me, y=(me["y"] + o // 16) % 4, z=(me["z"] + (o // 4) % 4) % 4, x=(me["x"] + o % 4) % 4)
-        pl.semaphore_signal(barrier, inc=1, device_id=to, device_id_type=MESH)
-        return 0
-
+    for axis in "yxz":
+        for dist in (1, 2, 3):
+            to = moved(me, **{axis: (me[axis] + dist) % 4})
+            pl.semaphore_signal(barrier, inc=1, device_id=to, device_id_type=MESH)
     pl.semaphore_signal(barrier, inc=1, device_id=other, device_id_type=MESH)
-    lax.fori_loop(1, 64, greet, 0)
 
     had[...] = hadamard(BLK)
     tile[...] = jnp.zeros_like(tile)
     tile[pl.ds(0, 128)] = idx[pl.ds(0, 128)]
     tile[pl.ds(128, 128)] = idx[pl.ds(128, 128)] ^ 2048
     tile[pl.ds(256, 128)] = idx[pl.ds(128, 128)]
-    pl.semaphore_wait(barrier, 64)
+    pl.semaphore_wait(barrier, 10)
 
     def core(i):
         if i == 8:
@@ -125,17 +123,61 @@
 
     lines = ((ly, "y", 0), (lz, "z", 1))
     planes = ((ly, pzy, "z", 0), (ly, pxy, "x", 1), (lz, pxz, "x", 2))
+    def core(i):
+        if i == 8:
+            return remote(sg, so, core_s.at[i], core_r.at[i], other)
+        place = pl.ds(i % 2 * 2048 + i // 2 * 512, 512)
+        return remote(x_hbm.at[place, pl.ds(128, 128)], xo.at[place, :], core_s.at[i], core_r.at[i], other)
+
+    def out_y(k, dist):
+        at = (me["y"] + dist) % 4
+        i = k * 3 + dist - 1
+        if k == 4:
+            src, dst = sg.at[rows(at * 8, 8), :], sy.at[rows(me["y"] * 8, 8), :]
+        else:
+            src = x_hbm.at[rows(at * 1024 + k * 256, 256), pl.ds(0, 128)]
+            dst = ry.at[me["y"], pl.ds(k * 256, 256), :]
+        return remote(src, dst, y_s.at[i], y_r.at[i], moved(me, y=at))
+
+    def back_y(k, dist):
+        at = (me["y"] + dist) % 4
+        i = 15 + k * 3 + dist - 1
+        return remote(
+            cy.at[at, pl.ds(k * 256, 256), :], dy.at[rows(me["y"] * 1024 + k * 256, 256), :],
+            y_s.at[i], y_r.at[i], moved(me, y=at),
+        )
+
+    def core_y(k):
+        i = 9 + k
+        if k == 4:
+            return remote(sy, syo, core_s.at[i], core_r.at[i], other)
+        place = pl.ds(k * 256, 256)
+        return remote(ry.at[:, place, :], ro.at[:, place, :], core_s.at[i], core_r.at[i], other)
+
+    def line(buf, axis, n, dist):
+        at = (me[axis] + dist) % 4
+        i = n * 3 + dist - 1
+        return remote(tile, buf.at[rows(me[axis] * 1024, 1024)], ix_s.at[i], ix_r.at[i], moved(me, **{axis: at}))
+
+    def plane(src, buf, axis, n, dist):
+        at = (me[axis] + dist) % 4
+        i = 6 + n * 3 + dist - 1
+        return remote(src, buf.at[rows(me[axis] * 4096, 4096)], ix_s.at[i], ix_r.at[i], moved(me, **{axis: at}))
+
+    lines = ((ly, "y", 0), (lz, "z", 1))
+    planes = ((ly, pzy, "z", 0), (ly, pxy, "x", 1), (lz, pxz, "x", 2))
     for buf, axis, n in lines:
         for dist in (1, 2, 3):
             line(buf, axis, n, dist).start()
         buf[rows(me[axis] * 1024, 1024)] = tile[...]
 
+    for dist in (1, 2, 3):
+        out_y(4, dist).start()
+        out_y(0, dist).start()
     core(8).start()
     for i in range(2):
         core(i).start()
-    for dist in (1, 2, 3):
-        out_y(4, dist).start()
-        out_y(0, dist).start()
+
     for i in range(2, 8):
         core(i).start()
     for k in range(1, 4):
@@ -246,8 +288,7 @@
 
         lax.fori_loop(0, 8, some, 0)
 
-    def pruned(part):
-        axis = PARTS[part][1]
+    def turned(part):
         arrive(1, part)
 
         def turn(i, _):
@@ -255,10 +296,12 @@
             return 0
 
         lax.fori_loop(0, 32, turn, 0)
-        for dist in (1, 2, 3):
-            gather(part, (me[axis] + dist) % 4, e)
+
+    def pruned(part, dist):
+        axis = PARTS[part][1]
+        gather(part, (me[axis] + dist) % 4, e if dist else f)
+        if dist:
             exchange(2, part, dist).start()
-        gather(part, me[axis], f)
 
     def cells(xs, zs):
         def cell(n, _):
@@ -373,8 +416,16 @@
     panel0(3)
     for i in range(3):
         to_smem(i).wait()
-    pruned(1)
-    pruned(3)
+    turned(1)
+    pruned(1, 1)
+    turned(3)
+    pruned(3, 1)
+    pruned(1, 2)
+    pruned(3, 2)
+    pruned(1, 3)
+    pruned(3, 3)
+    pruned(1, 0)
+    pruned(3, 0)
     pruned_y()
     scale = 1.0 / (128 * BLK) ** 0.5
     slot = lax.broadcasted_iota(jnp.int32, (128, 1), 0)
@@ -441,25 +492,6 @@
     gram(2, sk1, sk0)
     scatter(2)
     rb[rows((here * 4 + me["x"]) * 8, 8), :] = gp[rows(me["x"] * 128 + here * 8, 8), :]
-    each_piece(lambda p: p.wait_recv())
-    co[pl.ds(0, 8), :] = rb[...].reshape(64, 8, 128).sum(0)
-    swap = remote(co.at[pl.ds(0, 8), :], co.at[pl.ds(8, 8), :], core_s.at[14], core_r.at[14], other)
-    swap.start()
-    swap.wait_recv()
-    mine = pl.ds(pl.multiple_of(here * 8, 8), 8)
-    ob[mine, :] = (co[pl.ds(0, 8), :] + co[pl.ds(8, 8), :]) * (1.0 / (128 * 256))
-
-    def share(o):
-        to = {"y": (me["y"] + o // 4) % 4, "z": (me["z"] + o % 4) % 4}
-        return remote(ob.at[mine, :], ob.at[mine, :], ag_s.at[o], ag_r.at[o], moved(me, **to))
-
-    lax.fori_loop(1, 16, lambda o, _: (share(o).start(), 0)[1], 0)
-    lax.fori_loop(1, 16, lambda o, _: (share(o).wait_recv(), 0)[1], 0)
-    gr_out[...] = ob[...]
-
-    lax.fori_loop(1, 16, lambda o, _: (share(o).wait_send(), 0)[1], 0)
-    swap.wait_send()
-    each_piece(lambda p: p.wait_send())
     for i in range(9):
         core(i).wait_send()
     for k in range(5):
@@ -476,14 +508,29 @@
         for stage in range(4):
             for part in (1, 3) if stage < 2 else range(4):
                 exchange(stage, part, dist).wait_send()
-
-
-def hand_on(a, b, to_a, to_b, sem):
-    both = pltpu.make_async_copy(a, to_a, sem.at[0]), pltpu.make_async_copy(b, to_b, sem.at[1])
-    for copy in both:
-        copy.start()
-    for copy in both:
-        copy.wait()
+    each_piece(lambda p: p.wait_recv())
+    co[pl.ds(0, 8), :] = rb[...].reshape(64, 8, 128).sum(0)
+    swap = remote(co.at[pl.ds(0, 8), :], co.at[pl.ds(8, 8), :], core_s.at[14], core_r.at[14], other)
+    swap.start()
+    swap.wait_recv()
+    mine = pl.ds(pl.multiple_of(here * 8, 8), 8)
+    ob[mine, :] = (co[pl.ds(0, 8), :] + co[pl.ds(8, 8), :]) * (1.0 / (128 * 256))
+
+    def share(o):
+        to = {"y": (me["y"] + o // 4) % 4, "z": (me["z"] + o % 4) % 4}
+        return remote(ob.at[mine, :], ob.at[mine, :], ag_s.at[o], ag_r.at[o], moved(me, **to))
+
+    lax.fori_loop(1, 16, lambda o, _: (share(o).start(), 0)[1], 0)
+    swap.wait_send()
+    each_piece(lambda p: p.wait_send())
+    lax.fori_loop(1, 16, lambda o, _: (share(o).wait_send(), 0)[1], 0)
+    lax.fori_loop(1, 16, lambda o, _: (share(o).wait_recv(), 0)[1], 0)
+    gr_out[...] = ob[...]
+
+
+def hand_on(a, b, to_a, to_b):
+    to_a[...] = a[...]
+    to_b[...] = b[...]
 
 
 def local(matrix, signs, indices, counts):
@@ -515,14 +562,12 @@
             collective_id=0, has_side_effects=True, vmem_limit_bytes=56 * 2**20
         ),
     )(matrix, signs.reshape(32, 128), indices, counts)
-    anywhere = pl.BlockSpec(memory_space=pl.ANY)
     sketch, gram = pl.pallas_call(
         hand_on,
         name="hand_on",
         out_shape=(jax.ShapeDtypeStruct((256, 256), f32), jax.ShapeDtypeStruct((128, 128), f32)),
-        in_specs=[anywhere] * 2,
-        out_specs=(anywhere,) * 2,
-        scratch_shapes=[dma((2,))],
+        in_specs=[in_vmem] * 2,
+        out_specs=(in_vmem,) * 2,
     )(sketch, gram)
     return sketch, gram[None]
 

time: 122 us -> 105 us (0.86)
  Pallas kernels: 120 us -> 104 us
    pallas_call x1, Pallas kernels: 11 us -> 1.69 us  [local(): pl.pallas_call(hand_on, name='hand_on', out_shape=(jax.ShapeDtypeStruct((...]
    pallas_call x1, Pallas kernels: 109 us -> 102 us  [local(): pl.pallas_call(kernel, name='sketch_gram', out_shape=(jax.ShapeDtypeStruc...]
where the time goes in v5:
time: 105 us
  Pallas kernels  104 us (99%)
  between operations  1.28 us (1%)
    pallas_call x1, Pallas kernels, local(): pl.pallas_call(kernel, name='sketch_gram', out_shape=(jax.ShapeDtypeStruc...  102 us

profile of v5, /device:TPU:1, one launch (start us, length us, event | category | flops | bytes accessed | tf_op | source)
XLA Modules:
  0.0 104.9 jit_solution(2818574608420579237)
XLA Ops:
  1.3 101.9 %sketch_gram.1 = (f32[256,256]{1,0:T(8,128)}, f32[128,128]{1,0:T(8,128)}) custom-call(f32[4096,256]{1,0:T(8,128)} %x_hbm.1, s32[32,128]{1,0:T(8,128)} %bitcast.2, s32[256]{0:T(256)} %idx.1, s32[1]{0:T(128)S(6)} %copy.6.cnt), custom_call_target="tpu_custom_call" | custom-call | tf_op jit(solution)/shard_map/sketch_gram/pallas_call | solution.py:540
  103.2 1.7 %hand_on.1 = (f32[256,256]{1,0:T(8,128)}, f32[128,128]{1,0:T(8,128)}) custom-call(f32[256,256]{1,0:T(8,128)} %get-tuple-element.6.a, f32[128,128]{1,0:T(8,128)} %get-tuple-element.7.b), custom_call_target="tpu_custom_call" | custom-call | tf_op jit(solution)/shard_map/hand_on/pallas_call | solution.py:565

commit v6 on v5

--- a/solution.py
+++ b/solution.py
@@ -10,6 +10,7 @@
 MESH = pl.DeviceIdType.MESH
 BLK = 128
 HALF = 64
+FAR = (2, 1, 3)
 PARTS = (("y", "x", "z"), ("x", "z", "y"), ("y", "z", "x"), ("z", "x", "y"))
 
 
@@ -171,7 +172,7 @@
             line(buf, axis, n, dist).start()
         buf[rows(me[axis] * 1024, 1024)] = tile[...]
 
-    for dist in (1, 2, 3):
+    for dist in FAR:
         out_y(4, dist).start()
         out_y(0, dist).start()
     core(8).start()
@@ -181,7 +182,7 @@
     for i in range(2, 8):
         core(i).start()
     for k in range(1, 4):
-        for dist in (1, 2, 3):
+        for dist in FAR:
             out_y(k, dist).start()
 
     def exchange(stage, part, dist):
@@ -198,7 +199,7 @@
         return remote(src, dst, st_s.at[i], st_r.at[i], moved(me, **{axis: at}))
 
     def send(stage, part):
-        for dist in (1, 2, 3):
+        for dist in FAR:
             exchange(stage, part, dist).start()
 
     def arrive(stage, part):
@@ -230,7 +231,7 @@
             a[1, place, :] = jnp.where(lane, pltpu.roll(lo, HALF, 1), hi)
             return 0
 
-        lax.fori_loop(4 * j, 4 * j + 4, pair, 0)
+        lax.fori_loop(0, 4, lambda i, _: pair(4 * j + i, _), 0)
 
     def four(v):
         s, t, u, w = v[0] + v[1], v[0] - v[1], v[2] + v[3], v[2] - v[3]
@@ -249,7 +250,7 @@
             return 0
 
         lax.fori_loop(0, 2, step, 0)
-        for dist in (1, 2, 3):
+        for dist in FAR:
             back_y(k, dist).start()
         dy[rows(me["y"] * 1024 + k * 256, 256), :] = cy[me["y"], pl.ds(k * 256, 256), :]
 
@@ -303,10 +304,13 @@
         if dist:
             exchange(2, part, dist).start()
 
+    def far(n):
+        return jnp.where(n == 0, 2, jnp.where(n == 1, 1, jnp.where(n == 2, 3, 0)))
+
     def cells(xs, zs):
         def cell(n, _):
-            x = (me["x"] + (xs[0] + n if len(xs) > 1 else xs[0])) % 4
-            z = (me["z"] + (zs[0] + n if len(zs) > 1 else zs[0])) % 4
+            x = (me["x"] + far(xs[0] + n if len(xs) > 1 else xs[0])) % 4
+            z = (me["z"] + far(zs[0] + n if len(zs) > 1 else zs[0])) % 4
             base = (x * 4 + z) * 1024
             table = sxz
 
@@ -328,12 +332,12 @@
         for k in range(4):
             for dist in (1, 2, 3):
                 back_y(k, dist).wait_recv()
-        for dist in (1, 2, 3):
-            cells((dist,), range(dist, 5))
+        for n, dist in enumerate(FAR):
+            cells((n,), range(n, 4))
             exchange(2, 0, dist).start()
-            cells(range(dist + 1, 5), (dist,))
+            cells(range(n + 1, 4), (n,))
             exchange(2, 2, dist).start()
-        cells((4,), (4,))
+        cells((3,), (3,))
         for part in (0, 2):
             f[part, own(PARTS[part][1], 512), :] = e[part, own(PARTS[part][1], 512), :]
 
@@ -368,17 +372,13 @@
 
     load.wait()
     core(8).wait_recv()
-    for j in range(4):
-        core(2 * j).wait_recv()
-        core(2 * j + 1).wait_recv()
-        panel1(j)
-        for part in (1, 3):
-            axis = PARTS[part][0]
-
-            @pl.when(me[axis] != j)
-            def _():
-                exchange(0, part, (j - me[axis] + 4) % 4).start()
-
+    for i in range(8):
+        core(i).wait_recv()
+    for dist in FAR:
+        panel1((me["x"] + dist) % 4)
+        exchange(0, 1, dist).start()
+    panel1(me["x"])
+    send(0, 3)
     keep.wait()
     for dist in (1, 2, 3):
         out_y(4, dist).wait_recv()
@@ -417,11 +417,11 @@
     for i in range(3):
         to_smem(i).wait()
     turned(1)
+    pruned(1, 2)
+    turned(3)
+    pruned(3, 2)
     pruned(1, 1)
-    turned(3)
     pruned(3, 1)
-    pruned(1, 2)
-    pruned(3, 2)
     pruned(1, 3)
     pruned(3, 3)
     pruned(1, 0)
@@ -479,11 +479,11 @@
 
     last(1)
     last(3)
+    last(0)
+    last(2)
     sk1 = finish(1, 1, 3)
     gram(3, sk1, sk1)
     scatter(3)
-    last(0)
-    last(2)
     sk0 = finish(0, 0, 2)
     gram(0, sk0, sk0)
     scatter(0)

time: 105 us -> 99.1 us (0.944)
  Pallas kernels: 104 us -> 97.7 us
    pallas_call x1, Pallas kernels: 102 us -> 96 us  [local(): pl.pallas_call(kernel, name='sketch_gram', out_shape=(jax.ShapeDtypeStruc...]
where the time goes in v6:
time: 99.1 us; the launch traced here: 98.9 us
  Pallas kernels  97.7 us (99%)
  between operations  1.28 us (1%)
    pallas_call x1, Pallas kernels, local(): pl.pallas_call(kernel, name='sketch_gram', out_shape=(jax.ShapeDtypeStruc...  96 us

profile of v6, /device:TPU:1, one launch (start us, length us, event | category | flops | bytes accessed | tf_op | source)
XLA Modules:
  0.0 98.9 jit_solution(6160175450378562374)
XLA Ops:
  1.3 96.0 %sketch_gram.1 = (f32[256,256]{1,0:T(8,128)}, f32[128,128]{1,0:T(8,128)}) custom-call(f32[4096,256]{1,0:T(8,128)} %x_hbm.1, s32[32,128]{1,0:T(8,128)} %bitcast.2, s32[256]{0:T(256)} %idx.1, s32[1]{0:T(128)S(6)} %copy.6.cnt), custom_call_target="tpu_custom_call" | custom-call | tf_op jit(solution)/shard_map/sketch_gram/pallas_call | solution.py:540
  97.3 1.7 %hand_on.1 = (f32[256,256]{1,0:T(8,128)}, f32[128,128]{1,0:T(8,128)}) custom-call(f32[256,256]{1,0:T(8,128)} %get-tuple-element.6.a, f32[128,128]{1,0:T(8,128)} %get-tuple-element.7.b), custom_call_target="tpu_custom_call" | custom-call | tf_op jit(solution)/shard_map/hand_on/pallas_call | solution.py:565

commit v7 on v6

--- a/solution.py
+++ b/solution.py
@@ -42,7 +42,7 @@
 
 def kernel(
     x_hbm, sg, idx, cnt, sk_out, gr_out,
-    xm, xo, so, had, ry, ro, sy, syo, cy, dy, r, a, b, c, d1, d3, e, f, g, h,
+    xm, bo, had, ry, ro, sy, syo, cy, dy, r, a, b, c, d1, d3, e, f, g, h,
     tile, ly, lz, pzy, pxy, pxz, szy, sxy, sxz, gp, rb, co, ob,
     loc_sem, core_s, core_r, y_s, y_r, st_s, st_r, ix_s, ix_r, sm_sem, rs_s, rs_r, ag_s, ag_r,
 ):
@@ -79,13 +79,29 @@
     tile[pl.ds(0, 128)] = idx[pl.ds(0, 128)]
     tile[pl.ds(128, 128)] = idx[pl.ds(128, 128)] ^ 2048
     tile[pl.ds(256, 128)] = idx[pl.ds(128, 128)]
+
+    def split(v):
+        hi = v.astype(jnp.bfloat16)
+        return hi, (v - hi.astype(jnp.float32)).astype(jnp.bfloat16)
+
+    def times(left, v):
+        out = jnp.dot(left, jnp.concatenate(split(v), axis=1), preferred_element_type=jnp.float32)
+        return out[:, :128] + out[:, 128:]
+
+    def panel1(i, _):
+        def block(at):
+            left = had[...] * sg[pl.ds(at, 1), :].astype(jnp.float32)
+            return times(left.astype(jnp.bfloat16), xm[rows(at * BLK, BLK), :])
+
+        lo, hi = block(i), block(i + 16)
+        place = rows(i * BLK, BLK)
+        a[0, place, :] = jnp.where(lane, lo, pltpu.roll(hi, HALF, 1))
+        a[1, place, :] = jnp.where(lane, pltpu.roll(lo, HALF, 1), hi)
+        return 0
+
+    load.wait()
+    lax.fori_loop(0, 16, panel1, 0)
     pl.semaphore_wait(barrier, 10)
-
-    def core(i):
-        if i == 8:
-            return remote(sg, so, core_s.at[i], core_r.at[i], other)
-        place = pl.ds(i % 2 * 2048 + i // 2 * 512, 512)
-        return remote(x_hbm.at[place, pl.ds(128, 128)], xo.at[place, :], core_s.at[i], core_r.at[i], other)
 
     def out_y(k, dist):
         at = (me["y"] + dist) % 4
@@ -124,66 +140,6 @@
 
     lines = ((ly, "y", 0), (lz, "z", 1))
     planes = ((ly, pzy, "z", 0), (ly, pxy, "x", 1), (lz, pxz, "x", 2))
-    def core(i):
-        if i == 8:
-            return remote(sg, so, core_s.at[i], core_r.at[i], other)
-        place = pl.ds(i % 2 * 2048 + i // 2 * 512, 512)
-        return remote(x_hbm.at[place, pl.ds(128, 128)], xo.at[place, :], core_s.at[i], core_r.at[i], other)
-
-    def out_y(k, dist):
-        at = (me["y"] + dist) % 4
-        i = k * 3 + dist - 1
-        if k == 4:
-            src, dst = sg.at[rows(at * 8, 8), :], sy.at[rows(me["y"] * 8, 8), :]
-        else:
-            src = x_hbm.at[rows(at * 1024 + k * 256, 256), pl.ds(0, 128)]
-            dst = ry.at[me["y"], pl.ds(k * 256, 256), :]
-        return remote(src, dst, y_s.at[i], y_r.at[i], moved(me, y=at))
-
-    def back_y(k, dist):
-        at = (me["y"] + dist) % 4
-        i = 15 + k * 3 + dist - 1
-        return remote(
-            cy.at[at, pl.ds(k * 256, 256), :], dy.at[rows(me["y"] * 1024 + k * 256, 256), :],
-            y_s.at[i], y_r.at[i], moved(me, y=at),
-        )
-
-    def core_y(k):
-        i = 9 + k
-        if k == 4:
-            return remote(sy, syo, core_s.at[i], core_r.at[i], other)
-        place = pl.ds(k * 256, 256)
-        return remote(ry.at[:, place, :], ro.at[:, place, :], core_s.at[i], core_r.at[i], other)
-
-    def line(buf, axis, n, dist):
-        at = (me[axis] + dist) % 4
-        i = n * 3 + dist - 1
-        return remote(tile, buf.at[rows(me[axis] * 1024, 1024)], ix_s.at[i], ix_r.at[i], moved(me, **{axis: at}))
-
-    def plane(src, buf, axis, n, dist):
-        at = (me[axis] + dist) % 4
-        i = 6 + n * 3 + dist - 1
-        return remote(src, buf.at[rows(me[axis] * 4096, 4096)], ix_s.at[i], ix_r.at[i], moved(me, **{axis: at}))
-
-    lines = ((ly, "y", 0), (lz, "z", 1))
-    planes = ((ly, pzy, "z", 0), (ly, pxy, "x", 1), (lz, pxz, "x", 2))
-    for buf, axis, n in lines:
-        for dist in (1, 2, 3):
-            line(buf, axis, n, dist).start()
-        buf[rows(me[axis] * 1024, 1024)] = tile[...]
-
-    for dist in FAR:
-        out_y(4, dist).start()
-        out_y(0, dist).start()
-    core(8).start()
-    for i in range(2):
-        core(i).start()
-
-    for i in range(2, 8):
-        core(i).start()
-    for k in range(1, 4):
-        for dist in FAR:
-            out_y(k, dist).start()
 
     def exchange(stage, part, dist):
         axis = PARTS[part][max(stage - 1, 0)]
@@ -206,6 +162,29 @@
         for dist in (1, 2, 3):
             exchange(stage, part, dist).wait_recv()
 
+    def own(axis, size):
+        return rows(me[axis] * size, size)
+
+    def core_b(part, dist):
+        n, i = part // 2, part // 2 * 4 + dist
+        place = rows((me[PARTS[part][0]] - dist + 4) % 4 * 512, 512)
+        return remote(b.at[n, place, :], bo.at[n, place, :], core_s.at[i], core_r.at[i], other)
+
+    for dist in FAR:
+        out_y(4, dist).start()
+        out_y(0, dist).start()
+    for part in (1, 3):
+        send(0, part)
+        b[part // 2, own(PARTS[part][0], 512), :] = a[part // 2, own(PARTS[part][0], 512), :]
+        core_b(part, 0).start()
+    for buf, axis, n in lines:
+        for dist in (1, 2, 3):
+            line(buf, axis, n, dist).start()
+        buf[rows(me[axis] * 1024, 1024)] = tile[...]
+    for k in range(1, 4):
+        for dist in FAR:
+            out_y(k, dist).start()
+
     sign = (1 - 2 * me["c"]).astype(jnp.float32)
 
     def mixed(s0, s1, x0, x1):
@@ -213,25 +192,7 @@
         left = jnp.concatenate(
             [hm * (s0.astype(jnp.float32) * sign), hm * s1.astype(jnp.float32)], axis=1
         ).astype(jnp.bfloat16)
-        both = jnp.concatenate([x0, x1], axis=0)
-        hi = both.astype(jnp.bfloat16)
-        lo = (both - hi.astype(jnp.float32)).astype(jnp.bfloat16)
-        out = jnp.dot(left, jnp.concatenate([hi, lo], axis=1), preferred_element_type=jnp.float32)
-        return out[:, :128] + out[:, 128:]
-
-    def panel1(j):
-        def block(at):
-            place = rows(at * BLK, BLK)
-            return mixed(sg[pl.ds(at, 1), :], so[pl.ds(at, 1), :], xm[place, :], xo[place, :])
-
-        def pair(i, _):
-            lo, hi = block(i), block(i + 16)
-            place = rows(i * BLK, BLK)
-            a[0, place, :] = jnp.where(lane, lo, pltpu.roll(hi, HALF, 1))
-            a[1, place, :] = jnp.where(lane, pltpu.roll(lo, HALF, 1), hi)
-            return 0
-
-        lax.fori_loop(0, 4, lambda i, _: pair(4 * j + i, _), 0)
+        return times(left, jnp.concatenate([x0, x1], axis=0))
 
     def four(v):
         s, t, u, w = v[0] + v[1], v[0] - v[1], v[2] + v[3], v[2] - v[3]
@@ -259,17 +220,20 @@
             out_y(k, dist).wait_recv()
         core_y(k).start()
 
-    def own(axis, size):
-        return rows(me[axis] * size, size)
+    def across_b(part):
+        for dist in FAR:
+            exchange(0, part, dist).wait_recv()
+            core_b(part, dist).start()
 
     def whole(part):
         n, axis = part // 2, PARTS[part][0]
-        b[n, own(axis, 512), :] = a[n, own(axis, 512), :]
-        arrive(0, part)
+        for dist in range(4):
+            core_b(part, dist).wait_recv()
 
         def step(i, _):
-            for q, out in enumerate(four([b[n, rows(q * 512 + i * 32, 32), :] for q in range(4)])):
-                c[n, rows(q * 512 + i * 32, 32), :] = out
+            places = [rows(q * 512 + i * 32, 32) for q in range(4)]
+            for place, out in zip(places, four([b[n, p, :] * sign + bo[n, p, :] for p in places])):
+                c[n, place, :] = out
             return 0
 
         lax.fori_loop(0, 16, step, 0)
@@ -370,15 +334,6 @@
         arrive(3, part)
         return add_up(part, h, 128, PARTS[part][2])(0, 128)
 
-    load.wait()
-    core(8).wait_recv()
-    for i in range(8):
-        core(i).wait_recv()
-    for dist in FAR:
-        panel1((me["x"] + dist) % 4)
-        exchange(0, 1, dist).start()
-    panel1(me["x"])
-    send(0, 3)
     keep.wait()
     for dist in (1, 2, 3):
         out_y(4, dist).wait_recv()
@@ -396,6 +351,8 @@
     core_y(0).wait_recv()
     panel0(0)
     across(1)
+    across_b(1)
+    across_b(3)
     core_y(1).wait_recv()
     panel0(1)
     whole(1)
@@ -438,17 +395,14 @@
         hi = jnp.where(lane, pltpu.roll(p0, HALF, 1), p1) * scale
         sk_out[pl.ds(0, 128), cols] = jnp.where(slot < count, lo, 0.0)
         sk_out[pl.ds(128, 128), cols] = jnp.where(slot + 128 < count, hi, 0.0)
-        sk = sk_out[:, cols]
-        hi = sk.astype(jnp.bfloat16)
-        return hi, (sk - hi.astype(jnp.float32)).astype(jnp.bfloat16)
+        return jnp.concatenate(split(sk_out[:, cols]), axis=1)
 
     here = me["y"] * 4 + me["z"]
 
-    def gram(n, p, q):
-        def dot(u, v):
-            return lax.dot_general(u, v, (((0,), (0,)), ((), ())), preferred_element_type=jnp.float32)
-
-        gp[pl.ds(n * 128, 128), :] = dot(p[0], q[0]) + dot(p[0], q[1]) + dot(p[1], q[0])
+    def gram(p, q):
+        out = lax.dot_general(p, q, (((0,), (0,)), ((), ())), preferred_element_type=jnp.float32)
+        out = out[:128] + out[128:]
+        return [out[:, i : i + 128] + out[:, i + 128 : i + 256] for i in range(0, out.shape[1], 256)]
 
     def piece(dx, o):
         to = {"y": (me["y"] + o // 4) % 4, "z": (me["z"] + o % 4) % 4, "x": (me["x"] + dx) % 4}
@@ -482,18 +436,20 @@
     last(0)
     last(2)
     sk1 = finish(1, 1, 3)
-    gram(3, sk1, sk1)
+    gp[pl.ds(384, 128), :] = gram(sk1, sk1)[0]
     scatter(3)
     sk0 = finish(0, 0, 2)
-    gram(0, sk0, sk0)
+    first, second = gram(sk0, jnp.concatenate([sk0, sk1], axis=1))
+    gp[pl.ds(0, 128), :] = first
     scatter(0)
-    gram(1, sk0, sk1)
+    gp[pl.ds(128, 128), :] = second
     scatter(1)
-    gram(2, sk1, sk0)
+    gp[pl.ds(256, 128), :] = second.T
     scatter(2)
     rb[rows((here * 4 + me["x"]) * 8, 8), :] = gp[rows(me["x"] * 128 + here * 8, 8), :]
-    for i in range(9):
-        core(i).wait_send()
+    for part in (1, 3):
+        for dist in range(4):
+            core_b(part, dist).wait_send()
     for k in range(5):
         core_y(k).wait_send()
     for dist in (1, 2, 3):
@@ -544,7 +500,7 @@
         in_specs=[pl.BlockSpec(memory_space=pl.ANY), in_vmem, in_vmem, pl.BlockSpec(memory_space=smem)],
         out_specs=(in_vmem, in_vmem),
         scratch_shapes=[
-            vmem((4096, 128), f32), vmem((4096, 128), f32), vmem((32, 128), i32), vmem((128, 128), f32),
+            vmem((4096, 128), f32), vmem((2, 2048, 128), f32), vmem((128, 128), f32),
             vmem((4, 1024, 128), f32), vmem((4, 1024, 128), f32), vmem((32, 128), i32), vmem((32, 128), i32),
             vmem((4, 1024, 128), f32), vmem((4096, 128), f32), vmem((256, 128), f32),
             vmem((2, 2048, 128), f32), vmem((2, 2048, 128), f32), vmem((2, 2048, 128), f32),

time: 99.1 us -> 101 us (1.019)
  Pallas kernels: 97.7 us -> 99.9 us
    pallas_call x1, Pallas kernels: 96 us -> 98.2 us  [local(): pl.pallas_call(kernel, name='sketch_gram', out_shape=(jax.ShapeDtypeStruc...]
where the time goes in v7:
time: 101 us
  Pallas kernels  99.9 us (99%)
  between operations  1.28 us (1%)
    pallas_call x1, Pallas kernels, local(): pl.pallas_call(kernel, name='sketch_gram', out_shape=(jax.ShapeDtypeStruc...  98.2 us

profile of v7, /device:TPU:1, one launch (start us, length us, event | category | flops | bytes accessed | tf_op | source)
XLA Modules:
  0.0 101.1 jit_solution(15308375071304831350)
XLA Ops:
  1.3 98.2 %sketch_gram.1 = (f32[256,256]{1,0:T(8,128)}, f32[128,128]{1,0:T(8,128)}) custom-call(f32[4096,256]{1,0:T(8,128)} %x_hbm.1, s32[32,128]{1,0:T(8,128)} %bitcast.2, s32[256]{0:T(256)} %idx.1, s32[1]{0:T(128)S(6)} %copy.6.cnt), custom_call_target="tpu_custom_call" | custom-call | tf_op jit(solution)/shard_map/sketch_gram/pallas_call | solution.py:496
  99.5 1.7 %hand_on.1 = (f32[256,256]{1,0:T(8,128)}, f32[128,128]{1,0:T(8,128)}) custom-call(f32[256,256]{1,0:T(8,128)} %get-tuple-element.6.a, f32[128,128]{1,0:T(8,128)} %get-tuple-element.7.b), custom_call_target="tpu_custom_call" | custom-call | tf_op jit(solution)/shard_map/hand_on/pallas_call | solution.py:521

commit v8 on v7

--- a/solution.py
+++ b/solution.py
@@ -99,8 +99,6 @@
         a[1, place, :] = jnp.where(lane, pltpu.roll(lo, HALF, 1), hi)
         return 0
 
-    load.wait()
-    lax.fori_loop(0, 16, panel1, 0)
     pl.semaphore_wait(barrier, 10)
 
     def out_y(k, dist):
@@ -172,18 +170,22 @@
 
     for dist in FAR:
         out_y(4, dist).start()
+    for buf, axis, n in lines:
+        for dist in (1, 2, 3):
+            line(buf, axis, n, dist).start()
+    for dist in FAR:
         out_y(0, dist).start()
+    load.wait()
+    lax.fori_loop(0, 16, panel1, 0)
     for part in (1, 3):
         send(0, part)
         b[part // 2, own(PARTS[part][0], 512), :] = a[part // 2, own(PARTS[part][0], 512), :]
         core_b(part, 0).start()
-    for buf, axis, n in lines:
-        for dist in (1, 2, 3):
-            line(buf, axis, n, dist).start()
-        buf[rows(me[axis] * 1024, 1024)] = tile[...]
     for k in range(1, 4):
         for dist in FAR:
             out_y(k, dist).start()
+    for buf, axis, n in lines:
+        buf[rows(me[axis] * 1024, 1024)] = tile[...]
 
     sign = (1 - 2 * me["c"]).astype(jnp.float32)
 

time: 101 us -> 99.3 us (0.983)
  Pallas kernels: 99.9 us -> 97.8 us
    pallas_call x1, Pallas kernels: 98.2 us -> 96.1 us  [local(): pl.pallas_call(kernel, name='sketch_gram', out_shape=(jax.ShapeDtypeStruc...]
where the time goes in v8:
time: 99.3 us; the launch traced here: 99.1 us
  Pallas kernels  97.8 us (98%)
  between operations  1.28 us (1%)
    pallas_call x1, Pallas kernels, local(): pl.pallas_call(kernel, name='sketch_gram', out_shape=(jax.ShapeDtypeStruc...  96.1 us

profile of v8, /device:TPU:1, one launch (start us, length us, event | category | flops | bytes accessed | tf_op | source)
XLA Modules:
  0.0 99.1 jit_solution(4305678663357939158)
XLA Ops:
  1.3 96.1 %sketch_gram.1 = (f32[256,256]{1,0:T(8,128)}, f32[128,128]{1,0:T(8,128)}) custom-call(f32[4096,256]{1,0:T(8,128)} %x_hbm.1, s32[32,128]{1,0:T(8,128)} %bitcast.2, s32[256]{0:T(256)} %idx.1, s32[1]{0:T(128)S(6)} %copy.6.cnt), custom_call_target="tpu_custom_call" | custom-call | tf_op jit(solution)/shard_map/sketch_gram/pallas_call | solution.py:498
  97.4 1.7 %hand_on.1 = (f32[256,256]{1,0:T(8,128)}, f32[128,128]{1,0:T(8,128)}) custom-call(f32[256,256]{1,0:T(8,128)} %get-tuple-element.6.a, f32[128,128]{1,0:T(8,128)} %get-tuple-element.7.b), custom_call_target="tpu_custom_call" | custom-call | tf_op jit(solution)/shard_map/hand_on/pallas_call | solution.py:523

commit v9 on v8

--- a/solution.py
+++ b/solution.py
@@ -43,7 +43,7 @@
 def kernel(
     x_hbm, sg, idx, cnt, sk_out, gr_out,
     xm, bo, had, ry, ro, sy, syo, cy, dy, r, a, b, c, d1, d3, e, f, g, h,
-    tile, ly, lz, pzy, pxy, pxz, szy, sxy, sxz, gp, rb, co, ob,
+    tile, ly, lz, pzy, pxy, pxz, szy, sxy, sxz, gp, rb, ob,
     loc_sem, core_s, core_r, y_s, y_r, st_s, st_r, ix_s, ix_r, sm_sem, rs_s, rs_r, ag_s, ag_r,
 ):
     me = coords()
@@ -415,40 +415,19 @@
 
     def scatter(n):
         dx = (n - me["x"] + 4) % 4
-
-        def step(o, _):
+        for o in range(1, 16):
             piece(dx, o).start()
-            return 0
-
-        lax.fori_loop(1, 16, step, 0)
 
         @pl.when(dx != 0)
         def _():
             piece(dx, 0).start()
 
     def each_piece(act):
-        def step(n, _):
+        for n in range(1, 64):
             act(piece(n // 16, n % 16))
-            return 0
-
-        lax.fori_loop(1, 64, step, 0)
 
     last(1)
     last(3)
-    last(0)
-    last(2)
-    sk1 = finish(1, 1, 3)
-    gp[pl.ds(384, 128), :] = gram(sk1, sk1)[0]
-    scatter(3)
-    sk0 = finish(0, 0, 2)
-    first, second = gram(sk0, jnp.concatenate([sk0, sk1], axis=1))
-    gp[pl.ds(0, 128), :] = first
-    scatter(0)
-    gp[pl.ds(128, 128), :] = second
-    scatter(1)
-    gp[pl.ds(256, 128), :] = second.T
-    scatter(2)
-    rb[rows((here * 4 + me["x"]) * 8, 8), :] = gp[rows(me["x"] * 128 + here * 8, 8), :]
     for part in (1, 3):
         for dist in range(4):
             core_b(part, dist).wait_send()
@@ -464,26 +443,42 @@
         for k in range(4):
             back_y(k, dist).wait_send()
         for stage in range(4):
-            for part in (1, 3) if stage < 2 else range(4):
+            for part in (1, 3):
+                exchange(stage, part, dist).wait_send()
+    last(0)
+    last(2)
+    sk1 = finish(1, 1, 3)
+    gp[pl.ds(384, 128), :] = gram(sk1, sk1)[0]
+    scatter(3)
+    sk0 = finish(0, 0, 2)
+    first, second = gram(sk0, jnp.concatenate([sk0, sk1], axis=1))
+    gp[pl.ds(0, 128), :] = first
+    scatter(0)
+    gp[pl.ds(128, 128), :] = second
+    scatter(1)
+    gp[pl.ds(256, 128), :] = second.T
+    scatter(2)
+    rb[rows((here * 4 + me["x"]) * 8, 8), :] = gp[rows(me["x"] * 128 + here * 8, 8), :]
+    for dist in (1, 2, 3):
+        for stage in (2, 3):
+            for part in (0, 2):
                 exchange(stage, part, dist).wait_send()
     each_piece(lambda p: p.wait_recv())
-    co[pl.ds(0, 8), :] = rb[...].reshape(64, 8, 128).sum(0)
-    swap = remote(co.at[pl.ds(0, 8), :], co.at[pl.ds(8, 8), :], core_s.at[14], core_r.at[14], other)
-    swap.start()
-    swap.wait_recv()
-    mine = pl.ds(pl.multiple_of(here * 8, 8), 8)
-    ob[mine, :] = (co[pl.ds(0, 8), :] + co[pl.ds(8, 8), :]) * (1.0 / (128 * 256))
+    mine = rows(here * 8, 8)
+    ob[me["c"], mine, :] = rb[...].reshape(64, 8, 128).sum(0) * (1.0 / (128 * 256))
 
     def share(o):
-        to = {"y": (me["y"] + o // 4) % 4, "z": (me["z"] + o % 4) % 4}
-        return remote(ob.at[mine, :], ob.at[mine, :], ag_s.at[o], ag_r.at[o], moved(me, **to))
-
-    lax.fori_loop(1, 16, lambda o, _: (share(o).start(), 0)[1], 0)
-    swap.wait_send()
+        to = {"c": (me["c"] + o // 16) % 2, "y": (me["y"] + o // 4 % 4) % 4, "z": (me["z"] + o % 4) % 4}
+        piece_of = ob.at[me["c"], mine, :]
+        return remote(piece_of, piece_of, ag_s.at[o], ag_r.at[o], moved(me, **to))
+
+    for o in range(1, 32):
+        share(o).start()
     each_piece(lambda p: p.wait_send())
-    lax.fori_loop(1, 16, lambda o, _: (share(o).wait_send(), 0)[1], 0)
-    lax.fori_loop(1, 16, lambda o, _: (share(o).wait_recv(), 0)[1], 0)
-    gr_out[...] = ob[...]
+    for o in range(1, 32):
+        share(o).wait_send()
+        share(o).wait_recv()
+    gr_out[...] = ob[0] + ob[1]
 
 
 def hand_on(a, b, to_a, to_b):
@@ -512,9 +507,9 @@
             vmem((1024,), i32), vmem((4096,), i32), vmem((4096,), i32),
             vmem((16384,), i32), vmem((16384,), i32), vmem((16384,), i32),
             smem((16384,), i32), smem((16384,), i32), smem((16384,), i32),
-            vmem((512, 128), f32), vmem((512, 128), f32), vmem((16, 128), f32), vmem((128, 128), f32),
+            vmem((512, 128), f32), vmem((512, 128), f32), vmem((2, 128, 128), f32),
             dma((2,)), dma((15,)), dma((15,)), dma((27,)), dma((27,)), dma((48,)), dma((48,)),
-            dma((15,)), dma((15,)), dma((3,)), dma((64,)), dma((64,)), dma((16,)), dma((16,)),
+            dma((15,)), dma((15,)), dma((3,)), dma((64,)), dma((64,)), dma((32,)), dma((32,)),
         ],
         compiler_params=pltpu.CompilerParams(
             collective_id=0, has_side_effects=True, vmem_limit_bytes=56 * 2**20

time: 99.3 us -> 99.1 us (level)
  no operation moved by 1% of the time
where the time goes in v9:
time: 99.1 us; the launch traced here: 98.9 us
  Pallas kernels  97.7 us (99%)
  between operations  1.28 us (1%)
    pallas_call x1, Pallas kernels, local(): pl.pallas_call(kernel, name='sketch_gram', out_shape=(jax.ShapeDtypeStruc...  96 us

profile of v9, /device:TPU:1, one launch (start us, length us, event | category | flops | bytes accessed | tf_op | source)
XLA Modules:
  0.0 98.9 jit_solution(13117484460933319466)
XLA Ops:
  1.3 96.0 %sketch_gram.1 = (f32[256,256]{1,0:T(8,128)}, f32[128,128]{1,0:T(8,128)}) custom-call(f32[4096,256]{1,0:T(8,128)} %x_hbm.1, s32[32,128]{1,0:T(8,128)} %bitcast.2, s32[256]{0:T(256)} %idx.1, s32[1]{0:T(128)S(6)} %copy.6.cnt), custom_call_target="tpu_custom_call" | custom-call | tf_op jit(solution)/shard_map/sketch_gram/pallas_call | solution.py:493
  97.3 1.7 %hand_on.1 = (f32[256,256]{1,0:T(8,128)}, f32[128,128]{1,0:T(8,128)}) custom-call(f32[256,256]{1,0:T(8,128)} %get-tuple-element.6.a, f32[128,128]{1,0:T(8,128)} %get-tuple-element.7.b), custom_call_target="tpu_custom_call" | custom-call | tf_op jit(solution)/shard_map/hand_on/pallas_call | solution.py:518

commit v10 on v9

--- a/solution.py
+++ b/solution.py
@@ -103,38 +103,51 @@
 
     def out_y(k, dist):
         at = (me["y"] + dist) % 4
-        i = k * 3 + dist - 1
         if k == 4:
             src, dst = sg.at[rows(at * 8, 8), :], sy.at[rows(me["y"] * 8, 8), :]
         else:
             src = x_hbm.at[rows(at * 1024 + k * 256, 256), pl.ds(0, 128)]
             dst = ry.at[me["y"], pl.ds(k * 256, 256), :]
-        return remote(src, dst, y_s.at[i], y_r.at[i], moved(me, y=at))
+        return remote(src, dst, y_s.at[k], y_r.at[k], moved(me, y=at))
+
+    def all_out_y(k):
+        if k == 4:
+            return remote(sg.at[pl.ds(0, 24), :], sy.at[pl.ds(0, 24), :], y_s.at[k], y_r.at[k], other)
+        return remote(
+            x_hbm.at[pl.ds(0, 768), pl.ds(0, 128)], ry.at[0, pl.ds(0, 768), :], y_s.at[k], y_r.at[k], other
+        )
 
     def back_y(k, dist):
         at = (me["y"] + dist) % 4
-        i = 15 + k * 3 + dist - 1
         return remote(
             cy.at[at, pl.ds(k * 256, 256), :], dy.at[rows(me["y"] * 1024 + k * 256, 256), :],
-            y_s.at[i], y_r.at[i], moved(me, y=at),
+            y_s.at[5], y_r.at[5], moved(me, y=at),
         )
 
+    def all_back_y():
+        return remote(cy.at[pl.ds(0, 3)], ro.at[pl.ds(0, 3)], y_s.at[5], y_r.at[5], other)
+
     def core_y(k):
-        i = 9 + k
+        i = 2 + k
         if k == 4:
             return remote(sy, syo, core_s.at[i], core_r.at[i], other)
         place = pl.ds(k * 256, 256)
         return remote(ry.at[:, place, :], ro.at[:, place, :], core_s.at[i], core_r.at[i], other)
 
     def line(buf, axis, n, dist):
-        at = (me[axis] + dist) % 4
-        i = n * 3 + dist - 1
-        return remote(tile, buf.at[rows(me[axis] * 1024, 1024)], ix_s.at[i], ix_r.at[i], moved(me, **{axis: at}))
+        to = moved(me, **{axis: (me[axis] + dist) % 4})
+        return remote(tile, buf.at[rows(me[axis] * 1024, 1024)], ix_s.at[n], ix_r.at[n], to)
+
+    def all_line(buf, n):
+        return remote(lines[1 - n][0].at[pl.ds(0, 3072)], buf.at[pl.ds(0, 3072)], ix_s.at[n], ix_r.at[n], other)
 
     def plane(src, buf, axis, n, dist):
-        at = (me[axis] + dist) % 4
-        i = 6 + n * 3 + dist - 1
-        return remote(src, buf.at[rows(me[axis] * 4096, 4096)], ix_s.at[i], ix_r.at[i], moved(me, **{axis: at}))
+        to = moved(me, **{axis: (me[axis] + dist) % 4})
+        return remote(src, buf.at[rows(me[axis] * 4096, 4096)], ix_s.at[2 + n], ix_r.at[2 + n], to)
+
+    def all_plane(buf, n):
+        some = pl.ds(0, 12288)
+        return remote(planes[(n + 1) % 3][1].at[some], buf.at[some], ix_s.at[2 + n], ix_r.at[2 + n], other)
 
     lines = ((ly, "y", 0), (lz, "z", 1))
     planes = ((ly, pzy, "z", 0), (ly, pxy, "x", 1), (lz, pxz, "x", 2))
@@ -143,7 +156,7 @@
         axis = PARTS[part][max(stage - 1, 0)]
         at = (me[axis] + dist) % 4
         size = 128 if stage == 3 else 512
-        i = (stage * 4 + part) * 3 + dist - 1
+        i = stage * 4 + part
         src = (a, c, e, g)[stage].at[part // 2 if stage < 2 else part, rows(at * size, size), :]
         mine = rows(me[axis] * size, size)
         if stage == 1:
@@ -152,21 +165,25 @@
             dst = (b, None, f, h)[stage].at[part // 2 if stage < 2 else part, mine, :]
         return remote(src, dst, st_s.at[i], st_r.at[i], moved(me, **{axis: at}))
 
+    def all_three(stage, part):
+        n, i = part // 2 if stage < 2 else part, stage * 4 + part
+        three = pl.ds(0, 384 if stage == 3 else 1536)
+        dst = done[part].at[three, :] if stage == 1 else (b, None, f, h)[stage].at[n, three, :]
+        return remote((a, c, e, g)[stage].at[n, three, :], dst, st_s.at[i], st_r.at[i], other)
+
     def send(stage, part):
         for dist in FAR:
             exchange(stage, part, dist).start()
 
     def arrive(stage, part):
-        for dist in (1, 2, 3):
-            exchange(stage, part, dist).wait_recv()
+        all_three(stage, part).wait_recv()
 
     def own(axis, size):
         return rows(me[axis] * size, size)
 
-    def core_b(part, dist):
-        n, i = part // 2, part // 2 * 4 + dist
-        place = rows((me[PARTS[part][0]] - dist + 4) % 4 * 512, 512)
-        return remote(b.at[n, place, :], bo.at[n, place, :], core_s.at[i], core_r.at[i], other)
+    def core_b(part):
+        n = part // 2
+        return remote(b.at[n], bo.at[n], core_s.at[n], core_r.at[n], other)
 
     for dist in FAR:
         out_y(4, dist).start()
@@ -180,7 +197,6 @@
     for part in (1, 3):
         send(0, part)
         b[part // 2, own(PARTS[part][0], 512), :] = a[part // 2, own(PARTS[part][0], 512), :]
-        core_b(part, 0).start()
     for k in range(1, 4):
         for dist in FAR:
             out_y(k, dist).start()
@@ -218,19 +234,16 @@
         dy[rows(me["y"] * 1024 + k * 256, 256), :] = cy[me["y"], pl.ds(k * 256, 256), :]
 
     def across(k):
-        for dist in (1, 2, 3):
-            out_y(k, dist).wait_recv()
+        all_out_y(k).wait_recv()
         core_y(k).start()
 
     def across_b(part):
-        for dist in FAR:
-            exchange(0, part, dist).wait_recv()
-            core_b(part, dist).start()
+        arrive(0, part)
+        core_b(part).start()
 
     def whole(part):
         n, axis = part // 2, PARTS[part][0]
-        for dist in range(4):
-            core_b(part, dist).wait_recv()
+        core_b(part).wait_recv()
 
         def step(i, _):
             places = [rows(q * 512 + i * 32, 32) for q in range(4)]
@@ -295,9 +308,7 @@
         lax.fori_loop(0, max(len(xs), len(zs)), cell, 0)
 
     def pruned_y():
-        for k in range(4):
-            for dist in (1, 2, 3):
-                back_y(k, dist).wait_recv()
+        all_back_y().wait_recv()
         for n, dist in enumerate(FAR):
             cells((n,), range(n, 4))
             exchange(2, 0, dist).start()
@@ -337,14 +348,12 @@
         return add_up(part, h, 128, PARTS[part][2])(0, 128)
 
     keep.wait()
-    for dist in (1, 2, 3):
-        out_y(4, dist).wait_recv()
+    all_out_y(4).wait_recv()
     sy[own("y", 8), :] = sg[own("y", 8), :]
     core_y(4).start()
     across(0)
     for buf, axis, n in lines:
-        for dist in (1, 2, 3):
-            line(buf, axis, n, dist).wait_recv()
+        all_line(buf, n).wait_recv()
     for src, buf, axis, n in planes:
         for dist in (1, 2, 3):
             plane(src, buf, axis, n, dist).start()
@@ -367,8 +376,7 @@
         return pltpu.make_async_copy(planes[i][1], (szy, sxy, sxz)[i], sm_sem.at[i])
 
     for i, (src, buf, axis, n) in enumerate(planes):
-        for dist in (1, 2, 3):
-            plane(src, buf, axis, n, dist).wait_recv()
+        all_plane(buf, n).wait_recv()
         to_smem(i).start()
     across(3)
     core_y(3).wait_recv()
@@ -410,8 +418,7 @@
         to = {"y": (me["y"] + o // 4) % 4, "z": (me["z"] + o % 4) % 4, "x": (me["x"] + dx) % 4}
         src = to["x"] * 128 + (to["y"] * 4 + to["z"]) * 8
         dst = (here * 4 + me["x"]) * 8
-        n = dx * 16 + o
-        return remote(gp.at[rows(src, 8), :], rb.at[rows(dst, 8), :], rs_s.at[n], rs_r.at[n], moved(me, **to))
+        return remote(gp.at[rows(src, 8), :], rb.at[rows(dst, 8), :], rs_s.at[0], rs_r.at[0], moved(me, **to))
 
     def scatter(n):
         dx = (n - me["x"] + 4) % 4
@@ -422,29 +429,24 @@
         def _():
             piece(dx, 0).start()
 
-    def each_piece(act):
-        for n in range(1, 64):
-            act(piece(n // 16, n % 16))
+    def all_pieces():
+        most = pl.ds(0, 63 * 8)
+        return remote(gp.at[most, :], rb.at[most, :], rs_s.at[0], rs_r.at[0], other)
 
     last(1)
     last(3)
-    for part in (1, 3):
-        for dist in range(4):
-            core_b(part, dist).wait_send()
     for k in range(5):
         core_y(k).wait_send()
-    for dist in (1, 2, 3):
-        for buf, axis, n in lines:
-            line(buf, axis, n, dist).wait_send()
-        for src, buf, axis, n in planes:
-            plane(src, buf, axis, n, dist).wait_send()
-        for k in range(5):
-            out_y(k, dist).wait_send()
-        for k in range(4):
-            back_y(k, dist).wait_send()
+        all_out_y(k).wait_send()
+    all_back_y().wait_send()
+    for buf, axis, n in lines:
+        all_line(buf, n).wait_send()
+    for src, buf, axis, n in planes:
+        all_plane(buf, n).wait_send()
+    for part in (1, 3):
+        core_b(part).wait_send()
         for stage in range(4):
-            for part in (1, 3):
-                exchange(stage, part, dist).wait_send()
+            all_three(stage, part).wait_send()
     last(0)
     last(2)
     sk1 = finish(1, 1, 3)
@@ -459,26 +461,25 @@
     gp[pl.ds(256, 128), :] = second.T
     scatter(2)
     rb[rows((here * 4 + me["x"]) * 8, 8), :] = gp[rows(me["x"] * 128 + here * 8, 8), :]
-    for dist in (1, 2, 3):
-        for stage in (2, 3):
-            for part in (0, 2):
-                exchange(stage, part, dist).wait_send()
-    each_piece(lambda p: p.wait_recv())
-    mine = rows(here * 8, 8)
-    ob[me["c"], mine, :] = rb[...].reshape(64, 8, 128).sum(0) * (1.0 / (128 * 256))
+    for stage in (2, 3):
+        for part in (0, 2):
+            all_three(stage, part).wait_send()
+    all_pieces().wait_recv()
+    mine = rows(me["c"] * 128 + here * 8, 8)
+    ob[mine, :] = rb[...].reshape(64, 8, 128).sum(0) * (1.0 / (128 * 256))
 
     def share(o):
         to = {"c": (me["c"] + o // 16) % 2, "y": (me["y"] + o // 4 % 4) % 4, "z": (me["z"] + o % 4) % 4}
-        piece_of = ob.at[me["c"], mine, :]
-        return remote(piece_of, piece_of, ag_s.at[o], ag_r.at[o], moved(me, **to))
+        return remote(ob.at[mine, :], ob.at[mine, :], ag_s.at[0], ag_r.at[0], moved(me, **to))
 
     for o in range(1, 32):
         share(o).start()
-    each_piece(lambda p: p.wait_send())
-    for o in range(1, 32):
-        share(o).wait_send()
-        share(o).wait_recv()
-    gr_out[...] = ob[0] + ob[1]
+    all_pieces().wait_send()
+    most = pl.ds(0, 31 * 8)
+    shares = remote(rb.at[most, :], ob.at[most, :], ag_s.at[0], ag_r.at[0], other)
+    shares.wait_send()
+    shares.wait_recv()
+    gr_out[...] = ob[pl.ds(0, 128), :] + ob[pl.ds(128, 128), :]
 
 
 def hand_on(a, b, to_a, to_b):
@@ -507,9 +508,9 @@
             vmem((1024,), i32), vmem((4096,), i32), vmem((4096,), i32),
             vmem((16384,), i32), vmem((16384,), i32), vmem((16384,), i32),
             smem((16384,), i32), smem((16384,), i32), smem((16384,), i32),
-            vmem((512, 128), f32), vmem((512, 128), f32), vmem((2, 128, 128), f32),
-            dma((2,)), dma((15,)), dma((15,)), dma((27,)), dma((27,)), dma((48,)), dma((48,)),
-            dma((15,)), dma((15,)), dma((3,)), dma((64,)), dma((64,)), dma((32,)), dma((32,)),
+            vmem((512, 128), f32), vmem((512, 128), f32), vmem((256, 128), f32),
+            dma((2,)), dma((7,)), dma((7,)), dma((6,)), dma((6,)), dma((16,)), dma((16,)),
+            dma((5,)), dma((5,)), dma((3,)), dma((1,)), dma((1,)), dma((1,)), dma((1,)),
         ],
         compiler_params=pltpu.CompilerParams(
             collective_id=0, has_side_effects=True, vmem_limit_bytes=56 * 2**20

time: 99.1 us -> 96.3 us (0.972)
  Pallas kernels: 97.7 us -> 94.8 us
    pallas_call x1, Pallas kernels: 96 us -> 93.2 us  [local(): pl.pallas_call(kernel, name='sketch_gram', out_shape=(jax.ShapeDtypeStruc...]
where the time goes in v10:
time: 96.3 us; the launch traced here: 96.1 us
  Pallas kernels  94.8 us (98%)
  between operations  1.28 us (1%)
    pallas_call x1, Pallas kernels, local(): pl.pallas_call(kernel, name='sketch_gram', out_shape=(jax.ShapeDtypeStruc...  93.2 us

profile of v10, /device:TPU:1, one launch (start us, length us, event | category | flops | bytes accessed | tf_op | source)
XLA Modules:
  0.0 96.1 jit_solution(14386888288175564360)
XLA Ops:
  1.3 93.2 %sketch_gram.1 = (f32[256,256]{1,0:T(8,128)}, f32[128,128]{1,0:T(8,128)}) custom-call(f32[4096,256]{1,0:T(8,128)} %x_hbm.1, s32[32,128]{1,0:T(8,128)} %bitcast.2, s32[256]{0:T(256)} %idx.1, s32[1]{0:T(128)S(6)} %copy.6.cnt), custom_call_target="tpu_custom_call" | custom-call | tf_op jit(solution)/shard_map/sketch_gram/pallas_call | solution.py:494
  94.4 1.7 %hand_on.1 = (f32[256,256]{1,0:T(8,128)}, f32[128,128]{1,0:T(8,128)}) custom-call(f32[256,256]{1,0:T(8,128)} %get-tuple-element.6.a, f32[128,128]{1,0:T(8,128)} %get-tuple-element.7.b), custom_call_target="tpu_custom_call" | custom-call | tf_op jit(solution)/shard_map/hand_on/pallas_call | solution.py:519

commit v11 on v10

--- a/solution.py
+++ b/solution.py
@@ -43,7 +43,7 @@
 def kernel(
     x_hbm, sg, idx, cnt, sk_out, gr_out,
     xm, bo, had, ry, ro, sy, syo, cy, dy, r, a, b, c, d1, d3, e, f, g, h,
-    tile, ly, lz, pzy, pxy, pxz, szy, sxy, sxz, gp, rb, ob,
+    tile, ly, lz, pzy, pxy, pxz, szy, sxy, sxz, gp, rb, co, ob,
     loc_sem, core_s, core_r, y_s, y_r, st_s, st_r, ix_s, ix_r, sm_sem, rs_s, rs_r, ag_s, ag_r,
 ):
     me = coords()
@@ -414,24 +414,27 @@
         out = out[:128] + out[128:]
         return [out[:, i : i + 128] + out[:, i + 128 : i + 256] for i in range(0, out.shape[1], 256)]
 
+    odd = me["z"] % 2
+    nth = me["y"] * 2 + me["z"] // 2
+
     def piece(dx, o):
-        to = {"y": (me["y"] + o // 4) % 4, "z": (me["z"] + o % 4) % 4, "x": (me["x"] + dx) % 4}
-        src = to["x"] * 128 + (to["y"] * 4 + to["z"]) * 8
-        dst = (here * 4 + me["x"]) * 8
-        return remote(gp.at[rows(src, 8), :], rb.at[rows(dst, 8), :], rs_s.at[0], rs_r.at[0], moved(me, **to))
+        to = {"y": (me["y"] + o // 2) % 4, "z": (me["z"] // 2 + o % 2) % 2 * 2, "x": (me["x"] + dx) % 4}
+        src = to["x"] * 128 + (to["y"] * 2 + to["z"] // 2) * 16
+        dst = (here * 4 + me["x"]) * 16
+        return remote(gp.at[rows(src, 16), :], rb.at[rows(dst, 16), :], rs_s.at[0], rs_r.at[0], moved(me, **to))
 
     def scatter(n):
         dx = (n - me["x"] + 4) % 4
-        for o in range(1, 16):
+        for o in range(1, 8):
             piece(dx, o).start()
 
-        @pl.when(dx != 0)
+        @pl.when(dx + odd != 0)
         def _():
             piece(dx, 0).start()
 
-    def all_pieces():
-        most = pl.ds(0, 63 * 8)
-        return remote(gp.at[most, :], rb.at[most, :], rs_s.at[0], rs_r.at[0], other)
+    def pieces(count, of):
+        most = pl.ds(0, count * 16)
+        return remote(of.at[most, :], rb.at[most, :], rs_s.at[0], rs_r.at[0], other)
 
     last(1)
     last(3)
@@ -460,26 +463,41 @@
     scatter(1)
     gp[pl.ds(256, 128), :] = second.T
     scatter(2)
-    rb[rows((here * 4 + me["x"]) * 8, 8), :] = gp[rows(me["x"] * 128 + here * 8, 8), :]
     for stage in (2, 3):
         for part in (0, 2):
             all_three(stage, part).wait_send()
-    all_pieces().wait_recv()
-    mine = rows(me["c"] * 128 + here * 8, 8)
-    ob[mine, :] = rb[...].reshape(64, 8, 128).sum(0) * (1.0 / (128 * 256))
+    mine = rows(nth * 16, 16)
 
     def share(o):
-        to = {"c": (me["c"] + o // 16) % 2, "y": (me["y"] + o // 4 % 4) % 4, "z": (me["z"] + o % 4) % 4}
+        to = {"y": (me["y"] + o // 4) % 4, "z": (me["z"] + o % 4) % 4}
         return remote(ob.at[mine, :], ob.at[mine, :], ag_s.at[0], ag_r.at[0], moved(me, **to))
 
-    for o in range(1, 32):
-        share(o).start()
-    all_pieces().wait_send()
-    most = pl.ds(0, 31 * 8)
-    shares = remote(rb.at[most, :], ob.at[most, :], ag_s.at[0], ag_r.at[0], other)
-    shares.wait_send()
-    shares.wait_recv()
-    gr_out[...] = ob[pl.ds(0, 128), :] + ob[pl.ds(128, 128), :]
+    def shares(count):
+        most = pl.ds(0, count * 16)
+        return remote(rb.at[most, :], ob.at[most, :], ag_s.at[0], ag_r.at[0], other)
+
+    @pl.when(odd == 0)
+    def _():
+        rb[rows((here * 4 + me["x"]) * 16, 16), :] = gp[rows(me["x"] * 128 + nth * 16, 16), :]
+        pieces(63, rb).wait_recv()
+        co[pl.ds(0, 16), :] = rb[...].reshape(64, 16, 128).sum(0) * (1.0 / (128 * 256))
+        swap = remote(co.at[pl.ds(0, 16), :], co.at[pl.ds(16, 16), :], core_s.at[7], core_r.at[7], other)
+        swap.start()
+        swap.wait_recv()
+        ob[mine, :] = co[pl.ds(0, 16), :] + co[pl.ds(16, 16), :]
+        for o in range(1, 16):
+            share(o).start()
+        swap.wait_send()
+        pieces(31, gp).wait_send()
+        remote(rb.at[pl.ds(0, 240), :], rb.at[pl.ds(0, 240), :], ag_s.at[0], ag_r.at[0], other).wait_send()
+        shares(7).wait_recv()
+
+    @pl.when(odd != 0)
+    def _():
+        pieces(32, gp).wait_send()
+        shares(8).wait_recv()
+
+    gr_out[...] = ob[...]
 
 
 def hand_on(a, b, to_a, to_b):
@@ -508,8 +526,8 @@
             vmem((1024,), i32), vmem((4096,), i32), vmem((4096,), i32),
             vmem((16384,), i32), vmem((16384,), i32), vmem((16384,), i32),
             smem((16384,), i32), smem((16384,), i32), smem((16384,), i32),
-            vmem((512, 128), f32), vmem((512, 128), f32), vmem((256, 128), f32),
-            dma((2,)), dma((7,)), dma((7,)), dma((6,)), dma((6,)), dma((16,)), dma((16,)),
+            vmem((512, 128), f32), vmem((1024, 128), f32), vmem((32, 128), f32), vmem((128, 128), f32),
+            dma((2,)), dma((8,)), dma((8,)), dma((6,)), dma((6,)), dma((16,)), dma((16,)),
             dma((5,)), dma((5,)), dma((3,)), dma((1,)), dma((1,)), dma((1,)), dma((1,)),
         ],
         compiler_params=pltpu.CompilerParams(

time: 96.3 us -> 101 us (1.049)
  Pallas kernels: 94.8 us -> 99.9 us
    pallas_call x1, Pallas kernels: 93.2 us -> 98.2 us  [local(): pl.pallas_call(kernel, name='sketch_gram', out_shape=(jax.ShapeDtypeStruc...]
where the time goes in v11:
time: 101 us
  Pallas kernels  99.9 us (99%)
  between operations  1.28 us (1%)
    pallas_call x1, Pallas kernels, local(): pl.pallas_call(kernel, name='sketch_gram', out_shape=(jax.ShapeDtypeStruc...  98.2 us

profile of v11, /device:TPU:1, one launch (start us, length us, event | category | flops | bytes accessed | tf_op | source)
XLA Modules:
  0.0 101.1 jit_solution(5325661733494499976)
XLA Ops:
  1.3 98.2 %sketch_gram.1 = (f32[256,256]{1,0:T(8,128)}, f32[128,128]{1,0:T(8,128)}) custom-call(f32[4096,256]{1,0:T(8,128)} %x_hbm.1, s32[32,128]{1,0:T(8,128)} %bitcast.2, s32[256]{0:T(256)} %idx.1, s32[1]{0:T(128)S(6)} %copy.6.cnt), custom_call_target="tpu_custom_call" | custom-call | tf_op jit(solution)/shard_map/sketch_gram/pallas_call | solution.py:512
  99.5 1.7 %hand_on.1 = (f32[256,256]{1,0:T(8,128)}, f32[128,128]{1,0:T(8,128)}) custom-call(f32[256,256]{1,0:T(8,128)} %get-tuple-element.6.a, f32[128,128]{1,0:T(8,128)} %get-tuple-element.7.b), custom_call_target="tpu_custom_call" | custom-call | tf_op jit(solution)/shard_map/hand_on/pallas_call | solution.py:537

commit v12 on v10

--- a/solution.py
+++ b/solution.py
@@ -43,7 +43,7 @@
 def kernel(
     x_hbm, sg, idx, cnt, sk_out, gr_out,
     xm, bo, had, ry, ro, sy, syo, cy, dy, r, a, b, c, d1, d3, e, f, g, h,
-    tile, ly, lz, pzy, pxy, pxz, szy, sxy, sxz, gp, rb, ob,
+    tile, ly, lz, pzy, pxy, pxz, szy, sxy, sxz, gp, rb, co, ob,
     loc_sem, core_s, core_r, y_s, y_r, st_s, st_r, ix_s, ix_r, sm_sem, rs_s, rs_r, ag_s, ag_r,
 ):
     me = coords()
@@ -465,21 +465,26 @@
         for part in (0, 2):
             all_three(stage, part).wait_send()
     all_pieces().wait_recv()
-    mine = rows(me["c"] * 128 + here * 8, 8)
-    ob[mine, :] = rb[...].reshape(64, 8, 128).sum(0) * (1.0 / (128 * 256))
+    co[pl.ds(0, 8), :] = rb[...].reshape(64, 8, 128).sum(0) * (1.0 / (128 * 256))
+    swap = remote(co.at[pl.ds(0, 8), :], co.at[pl.ds(8, 8), :], core_s.at[7], core_r.at[7], other)
+    swap.start()
+    all_pieces().wait_send()
+    swap.wait_recv()
+    mine = rows(here * 8, 8)
+    ob[mine, :] = co[pl.ds(0, 8), :] + co[pl.ds(8, 8), :]
 
     def share(o):
-        to = {"c": (me["c"] + o // 16) % 2, "y": (me["y"] + o // 4 % 4) % 4, "z": (me["z"] + o % 4) % 4}
+        to = {"y": (me["y"] + o // 4) % 4, "z": (me["z"] + o % 4) % 4}
         return remote(ob.at[mine, :], ob.at[mine, :], ag_s.at[0], ag_r.at[0], moved(me, **to))
 
-    for o in range(1, 32):
+    for o in range(1, 16):
         share(o).start()
-    all_pieces().wait_send()
-    most = pl.ds(0, 31 * 8)
+    most = pl.ds(0, 15 * 8)
     shares = remote(rb.at[most, :], ob.at[most, :], ag_s.at[0], ag_r.at[0], other)
+    swap.wait_send()
     shares.wait_send()
     shares.wait_recv()
-    gr_out[...] = ob[pl.ds(0, 128), :] + ob[pl.ds(128, 128), :]
+    gr_out[...] = ob[...]
 
 
 def hand_on(a, b, to_a, to_b):
@@ -508,8 +513,8 @@
             vmem((1024,), i32), vmem((4096,), i32), vmem((4096,), i32),
             vmem((16384,), i32), vmem((16384,), i32), vmem((16384,), i32),
             smem((16384,), i32), smem((16384,), i32), smem((16384,), i32),
-            vmem((512, 128), f32), vmem((512, 128), f32), vmem((256, 128), f32),
-            dma((2,)), dma((7,)), dma((7,)), dma((6,)), dma((6,)), dma((16,)), dma((16,)),
+            vmem((512, 128), f32), vmem((512, 128), f32), vmem((16, 128), f32), vmem((128, 128), f32),
+            dma((2,)), dma((8,)), dma((8,)), dma((6,)), dma((6,)), dma((16,)), dma((16,)),
             dma((5,)), dma((5,)), dma((3,)), dma((1,)), dma((1,)), dma((1,)), dma((1,)),
         ],
         compiler_params=pltpu.CompilerParams(

time: 96.3 us -> 96.5 us (level)
  no operation moved by 1% of the time
where the time goes in v12:
time: 96.5 us; the launch traced here: 96.3 us
  Pallas kernels  95 us (98%)
  between operations  1.28 us (1%)
    pallas_call x1, Pallas kernels, local(): pl.pallas_call(kernel, name='sketch_gram', out_shape=(jax.ShapeDtypeStruc...  93.3 us

profile of v12, /device:TPU:1, one launch (start us, length us, event | category | flops | bytes accessed | tf_op | source)
XLA Modules:
  0.0 96.3 jit_solution(4107329613575674206)
XLA Ops:
  1.3 93.3 %sketch_gram.1 = (f32[256,256]{1,0:T(8,128)}, f32[128,128]{1,0:T(8,128)}) custom-call(f32[4096,256]{1,0:T(8,128)} %x_hbm.1, s32[32,128]{1,0:T(8,128)} %bitcast.2, s32[256]{0:T(256)} %idx.1, s32[1]{0:T(128)S(6)} %copy.6.cnt), custom_call_target="tpu_custom_call" | custom-call | tf_op jit(solution)/shard_map/sketch_gram/pallas_call | solution.py:499
  94.6 1.7 %hand_on.1 = (f32[256,256]{1,0:T(8,128)}, f32[128,128]{1,0:T(8,128)}) custom-call(f32[256,256]{1,0:T(8,128)} %get-tuple-element.6.a, f32[128,128]{1,0:T(8,128)} %get-tuple-element.7.b), custom_call_target="tpu_custom_call" | custom-call | tf_op jit(solution)/shard_map/hand_on/pallas_call | solution.py:524

commit v13 on v12

--- a/solution.py
+++ b/solution.py
@@ -429,9 +429,9 @@
         def _():
             piece(dx, 0).start()
 
-    def all_pieces():
-        most = pl.ds(0, 63 * 8)
-        return remote(gp.at[most, :], rb.at[most, :], rs_s.at[0], rs_r.at[0], other)
+    def pieces(count, of):
+        most = pl.ds(0, count * 8)
+        return remote(of.at[most, :], rb.at[most, :], rs_s.at[0], rs_r.at[0], other)
 
     last(1)
     last(3)
@@ -447,44 +447,66 @@
         core_b(part).wait_send()
         for stage in range(4):
             all_three(stage, part).wait_send()
-    last(0)
-    last(2)
     sk1 = finish(1, 1, 3)
     gp[pl.ds(384, 128), :] = gram(sk1, sk1)[0]
     scatter(3)
+    last(0)
+    last(2)
     sk0 = finish(0, 0, 2)
     first, second = gram(sk0, jnp.concatenate([sk0, sk1], axis=1))
     gp[pl.ds(0, 128), :] = first
     scatter(0)
     gp[pl.ds(128, 128), :] = second
     scatter(1)
-    gp[pl.ds(256, 128), :] = second.T
-    scatter(2)
     rb[rows((here * 4 + me["x"]) * 8, 8), :] = gp[rows(me["x"] * 128 + here * 8, 8), :]
     for stage in (2, 3):
         for part in (0, 2):
             all_three(stage, part).wait_send()
-    all_pieces().wait_recv()
-    co[pl.ds(0, 8), :] = rb[...].reshape(64, 8, 128).sum(0) * (1.0 / (128 * 256))
-    swap = remote(co.at[pl.ds(0, 8), :], co.at[pl.ds(8, 8), :], core_s.at[7], core_r.at[7], other)
-    swap.start()
-    all_pieces().wait_send()
-    swap.wait_recv()
     mine = rows(here * 8, 8)
-    ob[mine, :] = co[pl.ds(0, 8), :] + co[pl.ds(8, 8), :]
-
-    def share(o):
-        to = {"y": (me["y"] + o // 4) % 4, "z": (me["z"] + o % 4) % 4}
+
+    def share(o, x):
+        to = {"y": (me["y"] + o // 4) % 4, "z": (me["z"] + o % 4) % 4, "x": x}
         return remote(ob.at[mine, :], ob.at[mine, :], ag_s.at[0], ag_r.at[0], moved(me, **to))
 
-    for o in range(1, 16):
-        share(o).start()
-    most = pl.ds(0, 15 * 8)
-    shares = remote(rb.at[most, :], ob.at[most, :], ag_s.at[0], ag_r.at[0], other)
-    swap.wait_send()
-    shares.wait_send()
-    shares.wait_recv()
-    gr_out[...] = ob[...]
+    def shares(count):
+        most = pl.ds(0, count * 8)
+        return remote(rb.at[most, :], ob.at[most, :] if count < 17 else rb.at[most, :], ag_s.at[0], ag_r.at[0], other)
+
+    @pl.when(me["x"] != 2)
+    def _():
+        pieces(63, rb).wait_recv()
+        co[pl.ds(0, 8), :] = rb[...].reshape(64, 8, 128).sum(0) * (1.0 / (128 * 256))
+        swap = remote(co.at[pl.ds(0, 8), :], co.at[pl.ds(8, 8), :], core_s.at[7], core_r.at[7], other)
+        swap.start()
+        pieces(47, gp).wait_send()
+        swap.wait_recv()
+        ob[mine, :] = co[pl.ds(0, 8), :] + co[pl.ds(8, 8), :]
+
+        @pl.when(me["x"] == 1)
+        def _():
+            for o in range(16):
+                share(o, 2).start()
+
+        for o in range(1, 16):
+            share(o, me["x"]).start()
+        swap.wait_send()
+
+        @pl.when(me["x"] == 1)
+        def _():
+            shares(31).wait_send()
+
+        @pl.when(me["x"] != 1)
+        def _():
+            shares(15).wait_send()
+
+        shares(15).wait_recv()
+        gr_out[...] = ob[...]
+
+    @pl.when(me["x"] == 2)
+    def _():
+        pieces(48, gp).wait_send()
+        shares(16).wait_recv()
+        gr_out[...] = ob[...].T
 
 
 def hand_on(a, b, to_a, to_b):

time: 96.5 us -> 96.5 us (level)
  no operation moved by 1% of the time
where the time goes in v13:
time: 96.5 us; the launch traced here: 96.3 us
  Pallas kernels  95 us (98%)
  between operations  1.28 us (1%)
    pallas_call x1, Pallas kernels, local(): pl.pallas_call(kernel, name='sketch_gram', out_shape=(jax.ShapeDtypeStruc...  93.3 us

profile of v13, /device:TPU:1, one launch (start us, length us, event | category | flops | bytes accessed | tf_op | source)
XLA Modules:
  0.0 96.3 jit_solution(2153172339208095980)
XLA Ops:
  1.3 93.3 %sketch_gram.1 = (f32[256,256]{1,0:T(8,128)}, f32[128,128]{1,0:T(8,128)}) custom-call(f32[4096,256]{1,0:T(8,128)} %x_hbm.1, s32[32,128]{1,0:T(8,128)} %bitcast.2, s32[256]{0:T(256)} %idx.1, s32[1]{0:T(128)S(6)} %copy.6.cnt), custom_call_target="tpu_custom_call" | custom-call | tf_op jit(solution)/shard_map/sketch_gram/pallas_call | solution.py:521
  94.6 1.7 %hand_on.1 = (f32[256,256]{1,0:T(8,128)}, f32[128,128]{1,0:T(8,128)}) custom-call(f32[256,256]{1,0:T(8,128)} %get-tuple-element.6.a, f32[128,128]{1,0:T(8,128)} %get-tuple-element.7.b), custom_call_target="tpu_custom_call" | custom-call | tf_op jit(solution)/shard_map/hand_on/pallas_call | solution.py:546

commit v14 on v13

--- a/solution.py
+++ b/solution.py
@@ -11,6 +11,7 @@
 BLK = 128
 HALF = 64
 FAR = (2, 1, 3)
+FAR_PLANE = sorted(range(1, 16), key=lambda o: -(2 - abs(o // 4 - 2)) - (2 - abs(o % 4 - 2)))
 PARTS = (("y", "x", "z"), ("x", "z", "y"), ("y", "z", "x"), ("z", "x", "y"))
 
 
@@ -422,7 +423,7 @@
 
     def scatter(n):
         dx = (n - me["x"] + 4) % 4
-        for o in range(1, 16):
+        for o in FAR_PLANE:
             piece(dx, o).start()
 
         @pl.when(dx != 0)
@@ -484,10 +485,10 @@
 
         @pl.when(me["x"] == 1)
         def _():
-            for o in range(16):
+            for o in (*FAR_PLANE, 0):
                 share(o, 2).start()
 
-        for o in range(1, 16):
+        for o in FAR_PLANE:
             share(o, me["x"]).start()
         swap.wait_send()
 

time: 96.5 us -> 95.9 us (level)
  no operation moved by 1% of the time
where the time goes in v14:
time: 95.9 us; the launch traced here: 95.7 us
  Pallas kernels  94.4 us (98%)
  between operations  1.28 us (1%)
    pallas_call x1, Pallas kernels, local(): pl.pallas_call(kernel, name='sketch_gram', out_shape=(jax.ShapeDtypeStruc...  92.7 us

profile of v14, /device:TPU:1, one launch (start us, length us, event | category | flops | bytes accessed | tf_op | source)
XLA Modules:
  0.0 95.7 jit_solution(12572297085050691073)
XLA Ops:
  1.3 92.7 %sketch_gram.1 = (f32[256,256]{1,0:T(8,128)}, f32[128,128]{1,0:T(8,128)}) custom-call(f32[4096,256]{1,0:T(8,128)} %x_hbm.1, s32[32,128]{1,0:T(8,128)} %bitcast.2, s32[256]{0:T(256)} %idx.1, s32[1]{0:T(128)S(6)} %copy.6.cnt), custom_call_target="tpu_custom_call" | custom-call | tf_op jit(solution)/shard_map/sketch_gram/pallas_call | solution.py:522
  94.0 1.7 %hand_on.1 = (f32[256,256]{1,0:T(8,128)}, f32[128,128]{1,0:T(8,128)}) custom-call(f32[256,256]{1,0:T(8,128)} %get-tuple-element.6.a, f32[128,128]{1,0:T(8,128)} %get-tuple-element.7.b), custom_call_target="tpu_custom_call" | custom-call | tf_op jit(solution)/shard_map/hand_on/pallas_call | solution.py:547
